TPU v7x, 32 devices: a whole 2x2x4 slice. The times are simulated.
32 devices in a mesh: expert: 8 (over z, x), tensor: 4 (over y, core).
Axes of the slice: x: 2, y: 2, z: 4, core: 2. Of those that a mesh axis runs over, the one named last changes fastest.
Arguments:
- tokens: bfloat16 [2, 1024, 768], P(None, 'expert'), may hold values from -6 to 6
- out_grad: bfloat16 [2, 1024, 768], P(None, 'expert'), may hold values from -6 to 6
- routes: int32 [2, 1024, 2], P(None, 'expert'), may hold values from 0 to 7, as said below
- lengths: int32 [2, 7], replicated, may hold values from 1 to 512, 1024 in all within a row
- parents: int32 [2, 7], replicated, may hold values from 0 to 5, as said below
- attn_gain: bfloat16 [768], P('expert'), may hold values from 0.5 to 1.5
- ffn_gain: bfloat16 [768], P('expert'), may hold values from 0.5 to 1.5
- w_query: bfloat16 [768, 768], P('expert', 'tensor'), may hold values from -0.21875 to 0.21875
- w_key: bfloat16 [768, 768], P('expert', 'tensor'), may hold values from -0.21875 to 0.21875
- w_value: bfloat16 [768, 768], P('expert', 'tensor'), may hold values from -0.21875 to 0.21875
- w_out: bfloat16 [768, 768], P('tensor', 'expert'), may hold values from -0.875 to 0.875
- router: bfloat16 [768, 8], P('expert'), may hold values from -0.15625 to 0.15625
- shared_gate: bfloat16 [768, 2048], P('expert', 'tensor'), may hold values from -0.21875 to 0.21875
- shared_up: bfloat16 [768, 2048], P('expert', 'tensor'), may hold values from -0.21875 to 0.21875
- shared_down: bfloat16 [2048, 768], P('tensor', 'expert'), may hold values from -0.125 to 0.125
- expert_gate: bfloat16 [8, 768, 2048], P('expert', None, 'tensor'), may hold values from -0.21875 to 0.21875
- expert_up: bfloat16 [8, 768, 2048], P('expert', None, 'tensor'), may hold values from -0.21875 to 0.21875
- expert_down: bfloat16 [8, 2048, 768], P('expert', 'tensor'), may hold values from -0.125 to 0.125
Outputs:
- out: bfloat16 [2, 1024, 768], P(None, 'expert')
- grad_tokens: float32 [2, 1024, 768], P(None, 'expert')
- grad_attn_gain: float32 [768], P('expert')
- grad_ffn_gain: float32 [768], P('expert')
- grad_w_query: float32 [768, 768], P('expert', 'tensor')
- grad_w_key: float32 [768, 768], P('expert', 'tensor')
- grad_w_value: float32 [768, 768], P('expert', 'tensor')
- grad_w_out: float32 [768, 768], P('tensor', 'expert')
- grad_router: float32 [768, 8], P('expert')
- grad_shared_gate: float32 [768, 2048], P('expert', 'tensor')
- grad_shared_up: float32 [768, 2048], P('expert', 'tensor')
- grad_shared_down: float32 [2048, 768], P('tensor', 'expert')
- grad_expert_gate: float32 [8, 768, 2048], P('expert', None, 'tensor')
- grad_expert_up: float32 [8, 768, 2048], P('expert', None, 'tensor')
- grad_expert_down: float32 [8, 2048, 768], P('expert', 'tensor')
Inputs may be any that keep to these rules, and one draw needn't show every extreme that they name: In each aligned block of 128 rows of routes (the rows of one device in one micro-batch) the two experts of a token differ, no expert is named more than 64 times, and some expert is named exactly 64 times in every block. parents[m, s] < s for s >= 1 and parents[m, 0] = 0, so every path ends at segment 0; the last segment's parent is segment 7 - 2.
All inputs are finite; a program needn't handle non-finite values.
Results may differ from a plain program's by a relative error of at most 0.017.
Values may be sent and summed in bfloat16 or wider, within the bound.
A program may use at most 192 MiB of HBM per device.

v0:
```python
import math

import jax
import jax.numpy as jnp
from jax import lax
from jax.sharding import PartitionSpec as P

HEAD = 64


EPSILON = 1e-06
ROPE_BASE = 10000.0
KEY_BLOCK = 2048


def matmul(left, right):
    return jnp.dot(left, right, preferred_element_type=jnp.float32)


def tree_tables(lengths, parents):
    seg_count = lengths.shape[0]
    identity = jnp.arange(seg_count, dtype=jnp.int32)
    current = identity
    ancestry = jnp.zeros((seg_count, seg_count), jnp.float32)
    for depth_level in range(seg_count):
        chosen_mask = current[:, None] == identity[None, :]
        ancestry = jnp.maximum(ancestry, chosen_mask.astype(jnp.float32))
        current = jnp.sum(jnp.where(chosen_mask, parents[None, :], 0), axis=1)
    seg_ends = jnp.cumsum(lengths)
    starts = seg_ends - lengths
    sizes_float = lengths.astype(jnp.float32)
    offsets = jnp.sum(ancestry * sizes_float[None, :], axis=1) - sizes_float
    return (ancestry, starts, seg_ends, offsets)


def row_tables(row_ids, starts, seg_ends, offsets):
    member = (
        (row_ids[:, None] >= starts[None, :]) & (row_ids[:, None] < seg_ends[None, :])
    ).astype(jnp.float32)
    position_shift = offsets - starts.astype(jnp.float32)
    position = jnp.sum(member * position_shift[None, :], axis=1) + row_ids.astype(jnp.float32)
    return (member, position)


def rotary_tables(position, half_width):
    frequency = ROPE_BASE ** (-jnp.arange(half_width, dtype=jnp.float32) / half_width)
    angles = position[:, None] * frequency[None, :]
    return (jnp.cos(angles)[:, None, :], jnp.sin(angles)[:, None, :])


def rotate(head_values, position):
    half_width = head_values.shape[-1] // 2
    cosines, sine_values = rotary_tables(position, half_width)
    first_half = head_values[..., :half_width]
    second_half = head_values[..., half_width:]
    return jnp.concatenate(
        [
            first_half * cosines - second_half * sine_values,
            second_half * cosines + first_half * sine_values,
        ],
        axis=-1,
    )


def rotate_back(grad_heads, position):
    half_width = grad_heads.shape[-1] // 2
    cosines, sine_values = rotary_tables(position, half_width)
    first_half = grad_heads[..., :half_width]
    second_half = grad_heads[..., half_width:]
    return jnp.concatenate(
        [
            first_half * cosines + second_half * sine_values,
            second_half * cosines - first_half * sine_values,
        ],
        axis=-1,
    )


def silu_parts(gate_val):
    sigmoid_val = jax.nn.sigmoid(gate_val)
    return (gate_val * sigmoid_val, sigmoid_val * (1.0 + gate_val * (1.0 - sigmoid_val)))


def rms_back(grad_normed, source, norm_scale, gain):
    weighted = grad_normed * gain
    inner_mean = jnp.mean(weighted * source, axis=1, keepdims=True)
    return (
        norm_scale * weighted - norm_scale**3 * source * inner_mean,
        jnp.sum(grad_normed * source * norm_scale, axis=0),
    )


def visible(reach_rows, query_ids, key_member, key_ids):
    linked = matmul(reach_rows, key_member.T) > 0.5
    return linked & (key_ids[None, :] <= query_ids[:, None])


def score_block(query_heads, key_heads, seen, score_scale):
    scores = (
        jnp.einsum("qhd,khd->hqk", query_heads, key_heads, preferred_element_type=jnp.float32)
        * score_scale
    )
    return jnp.where(seen[None], jnp.exp(scores), 0.0)


def score_grads(weights_exp, grad_summed, value_heads, delta_rows):
    grad_exp = jnp.einsum(
        "qhd,khd->hqk", grad_summed, value_heads, preferred_element_type=jnp.float32
    )
    return (weights_exp * (grad_exp - jnp.transpose(delta_rows)[:, :, None])).astype(jnp.bfloat16)


def body(
    tokens,
    out_grad,
    routes,
    lengths,
    parents,
    attn_gain,
    ffn_gain,
    w_query,
    w_key,
    w_value,
    w_out,
    router,
    shared_gate,
    shared_up,
    shared_down,
    expert_gate,
    expert_up,
    expert_down,
):
    micro_count, row_count, model_width = tokens.shape
    devices = lax.axis_size("expert")
    tree_rows = row_count * devices
    expert_count = router.shape[1]
    owners = devices // expert_count
    capacity = 4 * row_count // expert_count
    score_scale = HEAD ** (-0.5)
    local_rows = lax.axis_index("expert") * row_count + jnp.arange(row_count, dtype=jnp.int32)
    part_gate = expert_gate[0]
    part_up = expert_up[0]
    part_down = expert_down[0]
    labels = jnp.arange(expert_count, dtype=jnp.int32)
    slot_ids = jnp.arange(expert_count * capacity, dtype=jnp.int32)
    pair_ids = jnp.arange(2 * row_count, dtype=jnp.int32)
    block_size = math.gcd(tree_rows, KEY_BLOCK)
    block_count = tree_rows // block_size
    layer_outputs = []
    token_gradients = []
    dense_sums = None
    expert_sums = None
    for micro_step in range(micro_count):
        gathered = (
            lax.all_gather(attn_gain, "expert", axis=0, tiled=True),
            lax.all_gather(ffn_gain, "expert", axis=0, tiled=True),
            lax.all_gather(w_query, "expert", axis=0, tiled=True),
            lax.all_gather(w_key, "expert", axis=0, tiled=True),
            lax.all_gather(w_value, "expert", axis=0, tiled=True),
            lax.all_gather(w_out, "expert", axis=1, tiled=True),
            lax.all_gather(router, "expert", axis=0, tiled=True),
            lax.all_gather(shared_gate, "expert", axis=0, tiled=True),
            lax.all_gather(shared_up, "expert", axis=0, tiled=True),
            lax.all_gather(shared_down, "expert", axis=1, tiled=True),
        )
        (
            gain_one,
            gain_two,
            query_weight,
            key_weight,
            value_weight,
            out_weight,
            router_weight,
            gate_weight,
            up_weight,
            down_weight,
        ) = gathered
        local_width = query_weight.shape[1]
        head_count = local_width // HEAD
        ancestry, starts, seg_ends, offsets = tree_tables(lengths[micro_step], parents[micro_step])
        member, position = row_tables(local_rows, starts, seg_ends, offsets)
        reach = matmul(member, ancestry)
        tokens_now = tokens[micro_step].astype(jnp.float32)
        norm_one = lax.rsqrt(jnp.mean(tokens_now * tokens_now, axis=1, keepdims=True) + EPSILON)
        normed_one = (tokens_now * norm_one * gain_one).astype(jnp.bfloat16)
        query_pre = matmul(normed_one, query_weight).reshape(row_count, head_count, HEAD)
        key_pre = matmul(normed_one, key_weight).reshape(row_count, head_count, HEAD)
        value_low = matmul(normed_one, value_weight).astype(jnp.bfloat16)
        queries = rotate(query_pre, position).astype(jnp.bfloat16)
        key_heads = rotate(key_pre, position).astype(jnp.bfloat16)
        key_value = jnp.concatenate([key_heads.reshape(row_count, local_width), value_low], axis=1)
        all_pairs = lax.all_gather(key_value, "expert", axis=0, tiled=True)

        def key_block_parts(block_index):
            first_key = block_index * block_size
            key_block = lax.dynamic_slice_in_dim(all_pairs, first_key, block_size, 0)
            key_ids = first_key + jnp.arange(block_size, dtype=jnp.int32)
            key_member, unused = row_tables(key_ids, starts, seg_ends, offsets)
            seen = visible(reach, local_rows, key_member, key_ids)
            block_keys = key_block[:, :local_width].reshape(block_size, head_count, HEAD)
            block_values = key_block[:, local_width:].reshape(block_size, head_count, HEAD)
            return (seen, block_keys, block_values)

        def forward_step(block_index, totals):
            seen, block_keys, block_values = key_block_parts(block_index)
            weights_exp = score_block(queries, block_keys, seen, score_scale)
            summed_part = jnp.einsum(
                "hqk,khd->qhd",
                weights_exp.astype(jnp.bfloat16),
                block_values,
                preferred_element_type=jnp.float32,
            )
            return (
                totals[0] + summed_part.reshape(row_count, local_width),
                totals[1] + jnp.transpose(jnp.sum(weights_exp, axis=2)),
            )

        initial = (
            jnp.zeros((row_count, local_width), jnp.float32),
            jnp.zeros((row_count, head_count), jnp.float32),
        )
        summed, row_total = lax.fori_loop(0, block_count, forward_step, initial)
        mixed = summed.reshape(row_count, head_count, HEAD) / row_total[:, :, None]
        mixed_low = mixed.reshape(row_count, local_width).astype(jnp.bfloat16)
        attn_out = lax.psum(matmul(mixed_low, out_weight), "tensor")
        residual = tokens_now + attn_out
        norm_two = lax.rsqrt(jnp.mean(residual * residual, axis=1, keepdims=True) + EPSILON)
        normed_two = (residual * norm_two * gain_two).astype(jnp.bfloat16)
        shared_g = matmul(normed_two, gate_weight)
        shared_u = matmul(normed_two, up_weight)
        shared_act, shared_slope = silu_parts(shared_g)
        shared_h = (shared_act * shared_u).astype(jnp.bfloat16)
        shared_y = matmul(shared_h, down_weight)
        logits = matmul(normed_two, router_weight)
        route_now = routes[micro_step]
        choose = (route_now[:, :, None] == labels[None, None, :]).astype(jnp.float32)
        gate_values = jax.nn.softmax(jnp.sum(choose * logits[:, None, :], axis=2), axis=1)
        flat_routes = route_now.reshape(2 * row_count)
        expert_hits = (flat_routes[:, None] == labels[None, :]).astype(jnp.int32)
        slot_rank = jnp.sum((jnp.cumsum(expert_hits, axis=0) - expert_hits) * expert_hits, axis=1)
        slot_index = flat_routes * capacity + slot_rank
        slot_match = slot_index[None, :] == slot_ids[:, None]
        filled = jnp.any(slot_match, axis=1)
        source = jnp.sum(jnp.where(slot_match, pair_ids[None, :], 0), axis=1)

        def to_owners(table, row_index):
            picked = jnp.take(table, row_index, axis=0)
            picked = jnp.where(filled[:, None], picked, jnp.zeros_like(picked))
            spread = jnp.broadcast_to(
                picked.reshape(expert_count, 1, capacity, model_width),
                (expert_count, owners, capacity, model_width),
            )
            return spread.reshape(devices, capacity, model_width)

        def from_owners(returned):
            merged = jnp.sum(
                returned.reshape(expert_count, owners, capacity, model_width), axis=1
            ).reshape(expert_count * capacity, model_width)
            return jnp.take(merged, slot_index, axis=0).reshape(row_count, 2, model_width)

        arrived = lax.all_to_all(
            to_owners(normed_two, source // 2), "expert", split_axis=0, concat_axis=0, tiled=True
        )
        slot_count = arrived.shape[1]
        flat_in = arrived.reshape(devices * slot_count, model_width)
        expert_g = matmul(flat_in, part_gate)
        expert_u = matmul(flat_in, part_up)
        expert_act, expert_unused = silu_parts(expert_g)
        expert_h = (expert_act * expert_u).astype(jnp.bfloat16)
        partial_out = matmul(expert_h, part_down).reshape(devices, slot_count, model_width)
        combined = lax.all_to_all(
            partial_out.astype(jnp.bfloat16), "expert", split_axis=0, concat_axis=0, tiled=True
        ).astype(partial_out.dtype)
        hidden_width = expert_g.shape[1]
        combined, arrived, kept_g, kept_u, kept_h = (
            combined,
            arrived,
            expert_g.reshape(devices, slot_count, hidden_width),
            expert_u.reshape(devices, slot_count, hidden_width),
            expert_h.reshape(devices, slot_count, hidden_width),
        )
        expert_y = from_owners(combined)
        cot_low = out_grad[micro_step]
        cotangent = cot_low.astype(jnp.float32)
        moe_part = jnp.sum(gate_values[:, :, None] * expert_y, axis=1)
        gate_dots = jnp.sum(cotangent[:, None, :] * expert_y, axis=2)
        ffn_out, grad_gate = (
            lax.psum((shared_y + moe_part).astype(jnp.bfloat16), "tensor").astype(jnp.float32),
            lax.psum(gate_dots.astype(jnp.bfloat16), "tensor").astype(jnp.float32),
        )
        layer_outputs.append((residual + ffn_out).astype(jnp.bfloat16))
        grad_shared_h = matmul(cot_low, down_weight.T)
        grad_shared_g = (grad_shared_h * shared_u * shared_slope).astype(jnp.bfloat16)
        grad_shared_u = (grad_shared_h * shared_act).astype(jnp.bfloat16)
        grad_chosen = gate_values * (
            grad_gate - jnp.sum(gate_values * grad_gate, axis=1, keepdims=True)
        )
        grad_logits = jnp.sum(choose * grad_chosen[:, :, None], axis=1).astype(jnp.bfloat16)
        grad_pairs_out = (
            (gate_values[:, :, None] * cotangent[:, None, :])
            .astype(jnp.bfloat16)
            .reshape(2 * row_count, model_width)
        )
        arrived_grad = lax.all_to_all(
            to_owners(grad_pairs_out, source), "expert", split_axis=0, concat_axis=0, tiled=True
        )
        slot_total = arrived_grad.shape[0] * arrived_grad.shape[1]
        flat_grad = arrived_grad.reshape(slot_total, model_width)
        flat_in = arrived.reshape(slot_total, model_width)
        hidden_width = kept_g.shape[2]
        expert_g = kept_g.reshape(slot_total, hidden_width)
        expert_u = kept_u.reshape(slot_total, hidden_width)
        expert_h = kept_h.reshape(slot_total, hidden_width)
        expert_act, expert_slope = silu_parts(expert_g)
        grad_hidden = matmul(flat_grad, part_down.T)
        grad_expert_g = (grad_hidden * expert_u * expert_slope).astype(jnp.bfloat16)
        grad_expert_u = (grad_hidden * expert_act).astype(jnp.bfloat16)
        grad_in = matmul(grad_expert_g, part_gate.T) + matmul(grad_expert_u, part_up.T)
        returned = lax.all_to_all(
            grad_in.reshape(arrived_grad.shape[0], arrived_grad.shape[1], model_width),
            "expert",
            split_axis=0,
            concat_axis=0,
            tiled=True,
        )
        normed_part = (
            matmul(grad_shared_g, gate_weight.T)
            + matmul(grad_shared_u, up_weight.T)
            + jnp.sum(from_owners(returned), axis=1)
        )
        grad_normed_two = lax.psum(normed_part, "tensor") + matmul(grad_logits, router_weight.T)
        grad_norm_part, grad_gain_two = rms_back(grad_normed_two, residual, norm_two, gain_two)
        grad_residual = cotangent + grad_norm_part
        grad_attn = grad_residual.astype(jnp.bfloat16)
        grad_mixed = matmul(grad_attn, out_weight.T).reshape(row_count, head_count, HEAD)
        grad_summed = (grad_mixed / row_total[:, :, None]).astype(jnp.bfloat16)
        delta_rows = jnp.sum(grad_mixed * mixed, axis=2) / row_total

        def block_terms(block_index):
            seen, block_keys, block_values = key_block_parts(block_index)
            weights_exp = score_block(queries, block_keys, seen, score_scale)
            grad_scores = score_grads(weights_exp, grad_summed, block_values, delta_rows)
            return (weights_exp, grad_scores, block_keys)

        zero_query = jnp.zeros((row_count, head_count, HEAD), jnp.float32)

        def key_step(gradient_query_weight, block_index):
            weights_exp, grad_scores, block_keys = block_terms(block_index)
            gradient_query_weight = (
                gradient_query_weight
                + jnp.einsum(
                    "hqk,khd->qhd", grad_scores, block_keys, preferred_element_type=jnp.float32
                )
                * score_scale
            )
            grad_keys = (
                jnp.einsum("hqk,qhd->khd", grad_scores, queries, preferred_element_type=jnp.float32)
                * score_scale
            )
            grad_values = jnp.einsum(
                "hqk,qhd->khd",
                weights_exp.astype(jnp.bfloat16),
                grad_summed,
                preferred_element_type=jnp.float32,
            )
            return (
                gradient_query_weight,
                jnp.concatenate(
                    [
                        grad_keys.reshape(block_size, local_width),
                        grad_values.reshape(block_size, local_width),
                    ],
                    axis=1,
                ),
            )

        gradient_query_weight, key_terms = lax.scan(
            key_step, zero_query, jnp.arange(block_count, dtype=jnp.int32)
        )
        grad_pairs = lax.psum_scatter(
            key_terms.reshape(tree_rows, 2 * local_width), "expert", scatter_dimension=0, tiled=True
        )
        grad_keys_rot = grad_pairs[:, :local_width].reshape(row_count, head_count, HEAD)
        grad_query_pre = (
            rotate_back(gradient_query_weight, position)
            .reshape(row_count, local_width)
            .astype(jnp.bfloat16)
        )
        grad_key_pre = (
            rotate_back(grad_keys_rot, position)
            .reshape(row_count, local_width)
            .astype(jnp.bfloat16)
        )
        grad_value_low = grad_pairs[:, local_width:].astype(jnp.bfloat16)
        normed_grad = (
            matmul(grad_query_pre, query_weight.T)
            + matmul(grad_key_pre, key_weight.T)
            + matmul(grad_value_low, value_weight.T)
        )
        grad_normed_one = lax.psum(normed_grad.astype(jnp.bfloat16), "tensor").astype(jnp.float32)
        grad_norm_first, grad_gain_one = rms_back(grad_normed_one, tokens_now, norm_one, gain_one)
        token_gradients.append(grad_residual + grad_norm_first)
        dense_step = (
            grad_gain_one,
            grad_gain_two,
            matmul(normed_one.T, grad_query_pre),
            matmul(normed_one.T, grad_key_pre),
            matmul(normed_one.T, grad_value_low),
            matmul(mixed_low.T, grad_attn),
            matmul(normed_two.T, grad_logits),
            matmul(normed_two.T, grad_shared_g),
            matmul(normed_two.T, grad_shared_u),
            matmul(shared_h.T, cot_low),
        )
        expert_step = (
            matmul(flat_in.T, grad_expert_g),
            matmul(flat_in.T, grad_expert_u),
            matmul(expert_h.T, flat_grad),
        )
        if dense_sums is None:
            dense_sums = dense_step
            expert_sums = expert_step
        else:
            dense_sums = tuple(
                (earlier + latest for earlier, latest in zip(dense_sums, dense_step))
            )
            expert_sums = tuple(
                (earlier + latest for earlier, latest in zip(expert_sums, expert_step))
            )
    final_gate, final_up, final_down = expert_sums
    reduced = (
        lax.psum_scatter(dense_sums[0], "expert", scatter_dimension=0, tiled=True),
        lax.psum_scatter(dense_sums[1], "expert", scatter_dimension=0, tiled=True),
        lax.psum_scatter(dense_sums[2], "expert", scatter_dimension=0, tiled=True),
        lax.psum_scatter(dense_sums[3], "expert", scatter_dimension=0, tiled=True),
        lax.psum_scatter(dense_sums[4], "expert", scatter_dimension=0, tiled=True),
        lax.psum_scatter(dense_sums[5], "expert", scatter_dimension=1, tiled=True),
        lax.psum_scatter(dense_sums[6], "expert", scatter_dimension=0, tiled=True),
        lax.psum_scatter(dense_sums[7], "expert", scatter_dimension=0, tiled=True),
        lax.psum_scatter(dense_sums[8], "expert", scatter_dimension=0, tiled=True),
        lax.psum_scatter(dense_sums[9], "expert", scatter_dimension=1, tiled=True),
    )
    return (
        jnp.stack(layer_outputs),
        jnp.stack(token_gradients),
        reduced[0],
        reduced[1],
        reduced[2],
        reduced[3],
        reduced[4],
        reduced[5],
        reduced[6],
        reduced[7],
        reduced[8],
        reduced[9],
        final_gate[None],
        final_up[None],
        final_down[None],
    )


def solution(mesh):
    in_specs = (
        P(None, "expert", None),
        P(None, "expert", None),
        P(None, "expert", None),
        P(),
        P(),
        P("expert"),
        P("expert"),
        P("expert", "tensor"),
        P("expert", "tensor"),
        P("expert", "tensor"),
        P("tensor", "expert"),
        P("expert", None),
        P("expert", "tensor"),
        P("expert", "tensor"),
        P("tensor", "expert"),
        P("expert", None, "tensor"),
        P("expert", None, "tensor"),
        P("expert", "tensor", None),
    )
    out_specs = (
        P(None, "expert", None),
        P(None, "expert", None),
        P("expert"),
        P("expert"),
        P("expert", "tensor"),
        P("expert", "tensor"),
        P("expert", "tensor"),
        P("tensor", "expert"),
        P("expert", None),
        P("expert", "tensor"),
        P("expert", "tensor"),
        P("tensor", "expert"),
        P("expert", None, "tensor"),
        P("expert", None, "tensor"),
        P("expert", "tensor", None),
    )
    return jax.shard_map(body, mesh=mesh, in_specs=in_specs, out_specs=out_specs, check_vma=False)
```

profile of v0, /device:TPU:0, one launch (start us, length us, event | category | flops | bytes accessed | tf_op | source)
XLA Modules:
  0.0 1389.8 jit_solution(17057167373491737223)
XLA Ops:
  7.3 33.1 %all_gather.48 = bf16[768,192]{1,0:T(8,128)(2,1)S(1)} all-gather(bf16[96,192]{1,0:T(8,128)(2,1)} %param.33), channel_id=1, replica_groups=mesh['expert'=8,'tensor'=4] {'expert'}, dimensions={0}, use_global_device_ids=true | all-gather | bytes 331776 | tf_op jit(solution)/shard_map/all_gather | solution.py:159
  45.4 21.4 %all-reduce.7 = (bf16[768]{0:T(1024)(128)(2,1)S(1)}, bf16[768]{0:T(1024)(128)(2,1)S(1)}) all-reduce(bf16[768]{0:T(1024)(128)(2,1)S(1)} %dynamic-update-slice, bf16[768]{0:T(1024)(128)(2,1)S(1)} %dynamic-update-slice.1), channel_id=1, replica_groups=mesh['expert'=8,'tensor'=4] {'expert'}, use_global_device_ids=true, to_apply=%add | all-reduce | flops 1536 | bytes 6144
  66.8 31.3 %all_gather.50 = bf16[768,192]{1,0:T(8,128)(2,1)S(1)} all-gather(bf16[96,192]{1,0:T(8,128)(2,1)} %param.31), channel_id=1, replica_groups=mesh['expert'=8,'tensor'=4] {'expert'}, dimensions={0}, use_global_device_ids=true | all-gather | bytes 331776 | tf_op jit(solution)/shard_map/all_gather | solution.py:157
  100.3 31.1 %all_gather.47 = bf16[768,192]{1,0:T(8,128)(2,1)S(1)} all-gather(bf16[96,192]{1,0:T(8,128)(2,1)S(1)} %copy-done.128), channel_id=1, replica_groups=mesh['expert'=8,'tensor'=4] {'expert'}, dimensions={0}, use_global_device_ids=true | all-gather | bytes 331776 | tf_op jit(solution)/shard_map/all_gather | solution.py:158
  137.0 28.1 %all_gather.57 = bf16[1024,384]{0,1:T(8,128)(2,1)S(1)} all-gather(bf16[128,384]{0,1:T(8,128)(2,1)S(1)} %pad_maximum_fusion.5), channel_id=1, replica_groups=mesh['expert'=8,'tensor'=4] {'expert'}, dimensions={0}, use_global_device_ids=true | all-gather | bytes 884736 | tf_op jit(solution)/shard_map/all_gather | solution.py:192
  165.4 31.4 %all_gather.51 = bf16[192,768]{0,1:T(8,128)(2,1)S(1)} all-gather(bf16[192,96]{0,1:T(8,128)(2,1)S(1)} %copy.64), channel_id=1, replica_groups=mesh['expert'=8,'tensor'=4] {'expert'}, dimensions={1}, use_global_device_ids=true | all-gather | bytes 331776 | tf_op jit(solution)/shard_map/all_gather | solution.py:160
  196.9 27.7 %all_gather.49 = bf16[1024,384]{0,1:T(8,128)(2,1)S(1)} all-gather(bf16[128,384]{0,1:T(8,128)(2,1)S(1)} %pad_maximum_fusion.4), channel_id=1, replica_groups=mesh['expert'=8,'tensor'=4] {'expert'}, dimensions={0}, use_global_device_ids=true | all-gather | bytes 884736 | tf_op jit(solution)/shard_map/all_gather | solution.py:192
  235.8 28.5 %all-reduce.16.cloned.1.call-done = (f32[128,768]{1,0:T(8,128)}, f32[128,768]{1,0:T(8,128)}) async-done(((f32[128,768]{1,0:T(8,128)}, f32[128,768]{1,0:T(8,128)}), (f32[128,768]{1,0:T(8,128)}, f32[128,768]{1,0:T(8,128)})) %all-reduce.16.cloned.1.call-update) | async-done | bytes 786448 | tf_op jit(solution)/shard_map/psum | solution.py:225
  270.1 5.5 all-to-all-start.2
  282.0 13.0 all-to-all-done.2
  295.0 4.0 all-to-all-start
  304.1 15.2 %all-to-all-done = bf16[8,64,768]{2,1,0:T(8,128)(2,1)S(1)} async-done(((bf16[8,64,768]{2,1,0:T(8,128)(2,1)}), bf16[8,64,768]{2,1,0:T(8,128)(2,1)S(1)}, u32[]{:S(2)}, u32[]{:S(2)}) %all-to-all-start) | async-done | bytes 786464 | tf_op jit(solution)/shard_map/all_to_all | solution.py:261
  319.3 4.2 all-to-all-start.3
  329.5 13.8 all-to-all-done.3
  343.4 4.2 all-to-all-start.1
  351.6 34.0 %all-gather = bf16[8,96,8]{1,2,0:T(8,128)(2,1)S(1)} all-gather(bf16[1,96,8]{1,2,0:T(8,128)(2,1)S(1)} %bitcast.475), channel_id=1, replica_groups=mesh['expert'=8,'tensor'=4] {'expert'}, dimensions={0}, use_global_device_ids=true | all-gather | bytes 13824 | tf_op jit(solution)/shard_map/all_gather | solution.py:161
  391.6 2.4 multiply_reduce_fusion
  398.3 2.6 multiply_reduce_fusion.1
  401.1 5.7 all-reduce.8
  408.9 2.7 gather_fusion.6
  411.6 2.3 select_select_fusion
  413.9 4.2 all-to-all-start.6
  423.7 14.9 %all-to-all-done.6 = bf16[8,64,768]{2,1,0:T(8,128)(2,1)} async-done(((bf16[8,64,768]{2,1,0:T(8,128)(2,1)}), bf16[8,64,768]{2,1,0:T(8,128)(2,1)}, u32[]{:S(2)}, u32[]{:S(2)}) %all-to-all-start.6) | async-done | bytes 786464 | tf_op jit(solution)/shard_map/all_to_all | solution.py:304
  438.6 4.2 all-to-all-start.4
  442.9 2.4 multiply_convert_fusion.2
  448.5 14.2 %all-to-all-done.4 = bf16[8,64,768]{2,1,0:T(8,128)(2,1)} async-done(((bf16[8,64,768]{2,1,0:T(8,128)(2,1)}), bf16[8,64,768]{2,1,0:T(8,128)(2,1)}, u32[]{:S(2)}, u32[]{:S(2)}) %all-to-all-start.4) | async-done | bytes 786464 | tf_op jit(solution)/shard_map/all_to_all | solution.py:304
  462.7 3.6 all-to-all-start.7
  466.3 59.4 %all_gather.53 = bf16[768,512]{1,0:T(8,128)(2,1)S(1)} all-gather(bf16[96,512]{1,0:T(8,128)(2,1)} %param.36), channel_id=1, replica_groups=mesh['expert'=8,'tensor'=4] {'expert'}, dimensions={0}, use_global_device_ids=true | all-gather | bytes 884736 | tf_op jit(solution)/shard_map/all_gather | solution.py:162
  525.8 34.6 %all_gather.54 = bf16[768,512]{1,0:T(8,128)(2,1)} all-gather(bf16[96,512]{1,0:T(8,128)(2,1)} %param.37), channel_id=1, replica_groups=mesh['expert'=8,'tensor'=4] {'expert'}, dimensions={0}, use_global_device_ids=true | all-gather | bytes 884736 | tf_op jit(solution)/shard_map/all_gather | solution.py:163
  560.3 2.5 multiply_convert_fusion.4
  566.1 4.3 all-to-all-start.5
  570.4 50.5 %all_gather.55 = bf16[512,768]{0,1:T(8,128)(2,1)S(1)} all-gather(bf16[512,96]{0,1:T(8,128)(2,1)} %param.38), channel_id=1, replica_groups=mesh['expert'=8,'tensor'=4] {'expert'}, dimensions={1}, use_global_device_ids=true | all-gather | bytes 884736 | tf_op jit(solution)/shard_map/all_gather | solution.py:164
  629.7 2.9 gather_fusion.5
  639.2 32.5 %all-reduce.14.cloned.1.call-done = (f32[128,768]{1,0:T(8,128)}, f32[128,768]{1,0:T(8,128)}) async-done(((f32[128,768]{1,0:T(8,128)}, f32[128,768]{1,0:T(8,128)}), (f32[128,768]{1,0:T(8,128)}, f32[128,768]{1,0:T(8,128)})) %all-reduce.14.cloned.1.call-update) | async-done | bytes 786448 | tf_op jit(solution)/shard_map/psum | solution.py:331
  703.0 43.1 %reduce-scatter.17.cloned.1.call-done = f32[128,384]{0,1:T(8,128)} async-done(((f32[1024,384]{0,1:T(8,128)}), f32[128,384]{0,1:T(8,128)}) %reduce-scatter.17.cloned.1.call-update) | async-done | bytes 196624 | tf_op jit(solution)/shard_map/reduce_scatter | solution.py:380
  748.1 67.0 %reduce-scatter.15.cloned.1.call-done = f32[128,384]{0,1:T(8,128)} async-done(((f32[1024,384]{0,1:T(8,128)}), f32[128,384]{0,1:T(8,128)}) %reduce-scatter.15.cloned.1.call-update) | async-done | bytes 196624 | tf_op jit(solution)/shard_map/reduce_scatter | solution.py:380
  828.4 50.7 %reduce-scatter.33.cloned.1.call-done = f32[96,8]{1,0:T(8,128)} async-done(((f32[768,8]{1,0:T(8,128)}), f32[96,8]{1,0:T(8,128)}) %reduce-scatter.33.cloned.1.call-update) | async-done | bytes 3088
  889.6 3.2 add_bitcast_fusion.1
  894.6 2.9 add_bitcast_fusion
  897.6 46.8 %reduce-scatter.31.cloned.1.call-done = f32[96,192]{1,0:T(8,128)} async-done(((f32[768,192]{1,0:T(8,128)}), f32[96,192]{1,0:T(8,128)}) %reduce-scatter.31.cloned.1.call-update) | async-done | bytes 73744
  947.7 33.3 %all-reduce.18.cloned.1.call-done = (bf16[128,768]{1,0:T(8,128)(2,1)}, bf16[128,768]{1,0:T(8,128)(2,1)}, bf16[128,768]{1,0:T(8,128)(2,1)}, bf16[128,768]{1,0:T(8,128)(2,1)}) async-done(((bf16[128,768]{1,0:T(8,128)(2,1)}, bf16[128,768]{1,0:T(8,128)(2,1)}, bf16[128,768]{1,0:T(8,128)(2,1)}, bf16[128,768]{1,0:T(8,128)(2,1)}), (bf16[128,768]{1,0:T(8,128)(2,1)}, bf16[128,768]{1,0:T(8,128)(2,1)}, ...) | async-done | bytes 786448 | tf_op jit(solution)/shard_map/psum | solution.py:288
  983.5 22.0 %all-reduce.4 = (f32[768]{0:T(1024)S(1)}, f32[768]{0:T(1024)S(1)}) all-reduce(f32[768]{0:T(1024)S(1)} %add.405, f32[768]{0:T(1024)S(1)} %add.406), channel_id=4, replica_groups=mesh['expert'=8,'tensor'=4] {'expert'}, use_global_device_ids=true, to_apply=%region_70.74.clone | all-reduce | flops 1536 | bytes 12288
  1008.8 41.9 %reduce-scatter.25.cloned.1.call-done = f32[96,512]{1,0:T(8,128)} async-done(((f32[768,512]{1,0:T(8,128)}), f32[96,512]{1,0:T(8,128)}) %reduce-scatter.25.cloned.1.call-update) | async-done | bytes 196624 | tf_op jit(solution)/shard_map/reduce_scatter | solution.py:439
  1050.7 67.8 %reduce-scatter.27.cloned.1.call-done = f32[96,512]{1,0:T(8,128)} async-done(((f32[768,512]{1,0:T(8,128)}), f32[96,512]{1,0:T(8,128)}) %reduce-scatter.27.cloned.1.call-update) | async-done | bytes 196624 | tf_op jit(solution)/shard_map/reduce_scatter | solution.py:440
  1118.5 68.0 %reduce-scatter.29.cloned.1.call-done = f32[512,96]{0,1:T(8,128)} async-done(((f32[512,768]{0,1:T(8,128)}), f32[512,96]{0,1:T(8,128)}) %reduce-scatter.29.cloned.1.call-update) | async-done | bytes 196624 | tf_op jit(solution)/shard_map/reduce_scatter | solution.py:441
  1186.5 65.4 %reduce-scatter.19.cloned.1.call-done = f32[96,192]{1,0:T(8,128)} async-done(((f32[768,192]{1,0:T(8,128)}), f32[96,192]{1,0:T(8,128)}) %reduce-scatter.19.cloned.1.call-update) | async-done | bytes 73744 | tf_op jit(solution)/shard_map/reduce_scatter | solution.py:434
  1251.9 65.6 %reduce-scatter.21.cloned.1.call-done = f32[96,192]{1,0:T(8,128)} async-done(((f32[768,192]{1,0:T(8,128)}), f32[96,192]{1,0:T(8,128)}) %reduce-scatter.21.cloned.1.call-update) | async-done | bytes 73744 | tf_op jit(solution)/shard_map/reduce_scatter | solution.py:435
  1317.5 65.4 %reduce-scatter.23.cloned.1.call-done = f32[96,192]{1,0:T(8,128)} async-done(((f32[768,192]{1,0:T(8,128)}), f32[96,192]{1,0:T(8,128)}) %reduce-scatter.23.cloned.1.call-update) | async-done | bytes 73744 | tf_op jit(solution)/shard_map/reduce_scatter | solution.py:436
  (646 shorter events, 155.8 us)
Async XLA Ops:
  7.2 295.4 %copy-start = (bf16[1,512,768]{2,1,0:T(8,128)(2,1)S(1)}, bf16[1,512,768]{2,1,0:T(8,128)(2,1)}, u32[]{:S(2)}) copy-start(bf16[1,512,768]{2,1,0:T(8,128)(2,1)} %param.41) | copy-start | bytes 2359300
  7.2 91.7 %copy-start.3 = (bf16[2,128,768]{2,1,0:T(8,128)(2,1)S(1)}, bf16[2,128,768]{2,1,0:T(8,128)(2,1)}, u32[]{:S(2)}) copy-start(bf16[2,128,768]{2,1,0:T(8,128)(2,1)} %param.24) | copy-start | bytes 1179652
  7.2 257.1 %all-reduce.16.cloned.1.call-start = ((), (), s32[]{:S(2)}) async-start(), calls=%async_computation.29 | async-start | bytes 1572864 | tf_op jit(solution)/shard_map/psum | solution.py:225
  40.4 59.6 %copy-start.39 = (bf16[768,192]{1,0:T(8,128)(2,1)}, bf16[768,192]{1,0:T(8,128)(2,1)S(1)}, u32[]{:S(2)}) copy-start(bf16[768,192]{1,0:T(8,128)(2,1)S(1)} %all_gather.48) | copy-start | bytes 884740
  136.4 60.4 %copy-start.110 = (f32[128,32]{0,1:T(8,128)}, f32[128,32]{0,1:T(8,128)S(1)}, u32[]{:S(2)}) copy-start(f32[128,32]{0,1:T(8,128)S(1)} %get-tuple-element.248) | copy-start | bytes 49156
  136.4 60.3 %copy-start.112 = (f32[128,32]{0,1:T(8,128)}, f32[128,32]{0,1:T(8,128)S(1)}, u32[]{:S(2)}) copy-start(f32[128,32]{0,1:T(8,128)S(1)} %get-tuple-element.249) | copy-start | bytes 49156
  136.5 88.1 %copy-start.122 = (bf16[128,3,32]{0,2,1:T(8,128)(2,1)}, bf16[128,3,32]{0,2,1:T(8,128)(2,1)S(1)}, u32[]{:S(2)}) copy-start(bf16[128,3,32]{0,2,1:T(8,128)(2,1)S(1)} %get-tuple-element.226) | copy-start | bytes 73732
  136.5 88.1 %copy-start.124 = (bf16[128,3,32]{0,2,1:T(8,128)(2,1)}, bf16[128,3,32]{0,2,1:T(8,128)(2,1)S(1)}, u32[]{:S(2)}) copy-start(bf16[128,3,32]{0,2,1:T(8,128)(2,1)S(1)} %get-tuple-element.227) | copy-start | bytes 73732
  165.2 59.4 %copy-start.63 = (bf16[1024,192]{0,1:T(8,128)(2,1)}, bf16[1024,192]{0,1:T(8,128)(2,1)S(1)}, u32[]{:S(2)}) copy-start(bf16[1024,192]{0,1:T(8,128)(2,1)S(1)} %get-tuple-element.198) | copy-start | bytes 1179652
  165.3 60.1 %copy-start.42 = (bf16[1024,192]{0,1:T(8,128)(2,1)}, bf16[1024,192]{0,1:T(8,128)(2,1)S(1)}, u32[]{:S(2)}) copy-start(bf16[1024,192]{0,1:T(8,128)(2,1)S(1)} %get-tuple-element.199) | copy-start | bytes 1179652
  270.1 24.9 %all-to-all-start.2 = ((bf16[8,64,768]{2,1,0:T(8,128)(2,1)}), bf16[8,64,768]{2,1,0:T(8,128)(2,1)S(1)}, u32[]{:S(2)}, u32[]{:S(2)}) async-start(bf16[8,64,768]{2,1,0:T(8,128)(2,1)} %bitcast.55), calls=%async_computation.2 | async-start | bytes 1572864 | tf_op jit(solution)/shard_map/all_to_all | solution.py:261
  295.0 24.3 %all-to-all-start = ((bf16[8,64,768]{2,1,0:T(8,128)(2,1)}), bf16[8,64,768]{2,1,0:T(8,128)(2,1)S(1)}, u32[]{:S(2)}, u32[]{:S(2)}) async-start(bf16[8,64,768]{2,1,0:T(8,128)(2,1)} %bitcast.427), calls=%async_computation | async-start | bytes 1572864 | tf_op jit(solution)/shard_map/all_to_all | solution.py:261
  319.3 24.1 %all-to-all-start.3 = ((bf16[8,64,768]{2,1,0:T(8,128)(2,1)}), bf16[8,64,768]{2,1,0:T(8,128)(2,1)}, u32[]{:S(2)}, u32[]{:S(2)}) async-start(bf16[8,64,768]{2,1,0:T(8,128)(2,1)} %convolution_convert_fusion), calls=%async_computation.3 | async-start | bytes 1572864 | tf_op jit(solution)/shard_map/all_to_all | solution.py:271
  343.4 51.4 %all-to-all-start.1 = ((bf16[8,64,768]{2,1,0:T(8,128)(2,1)}), bf16[8,64,768]{2,1,0:T(8,128)(2,1)}, u32[]{:S(2)}, u32[]{:S(2)}) async-start(bf16[8,64,768]{2,1,0:T(8,128)(2,1)} %convolution_convert_fusion.1), calls=%async_computation.1 | async-start | bytes 1572864 | tf_op jit(solution)/shard_map/all_to_all | solution.py:271
  413.9 24.7 %all-to-all-start.6 = ((bf16[8,64,768]{2,1,0:T(8,128)(2,1)}), bf16[8,64,768]{2,1,0:T(8,128)(2,1)}, u32[]{:S(2)}, u32[]{:S(2)}) async-start(bf16[8,64,768]{2,1,0:T(8,128)(2,1)} %bitcast.426), calls=%async_computation.7 | async-start | bytes 1572864 | tf_op jit(solution)/shard_map/all_to_all | solution.py:304
  438.6 24.1 %all-to-all-start.4 = ((bf16[8,64,768]{2,1,0:T(8,128)(2,1)}), bf16[8,64,768]{2,1,0:T(8,128)(2,1)}, u32[]{:S(2)}, u32[]{:S(2)}) async-start(bf16[8,64,768]{2,1,0:T(8,128)(2,1)} %bitcast.61), calls=%async_computation.4 | async-start | bytes 1572864 | tf_op jit(solution)/shard_map/all_to_all | solution.py:304
  462.7 103.4 %all-to-all-start.7 = ((f32[8,64,768]{2,1,0:T(8,128)}), f32[8,64,768]{2,1,0:T(8,128)S(1)}, u32[]{:S(2)}, u32[]{:S(2)}) async-start(f32[8,64,768]{2,1,0:T(8,128)} %bitcast.418), calls=%async_computation.8 | async-start | bytes 3145728 | tf_op jit(solution)/shard_map/all_to_all | solution.py:319
  466.3 94.0 %copy-start.69 = (f32[512,512]{1,0:T(8,128)S(1)}, f32[512,512]{1,0:T(8,128)}, u32[]{:S(2)}) copy-start(f32[512,512]{1,0:T(8,128)} %copy-done.68) | copy-start | bytes 3145732
  566.1 63.6 %all-to-all-start.5 = ((f32[8,64,768]{2,1,0:T(8,128)}), f32[8,64,768]{2,1,0:T(8,128)}, u32[]{:S(2)}, u32[]{:S(2)}) async-start(f32[8,64,768]{2,1,0:T(8,128)} %bitcast.417), calls=%async_computation.5 | async-start | bytes 3145728 | tf_op jit(solution)/shard_map/all_to_all | solution.py:319
  570.4 51.2 %copy-start.2 = (bf16[768,512]{1,0:T(8,128)(2,1)S(1)}, bf16[768,512]{1,0:T(8,128)(2,1)}, u32[]{:S(2)}) copy-start(bf16[768,512]{1,0:T(8,128)(2,1)} %all_gather.54) | copy-start | bytes 2359300
  570.4 101.4 %all-reduce.14.cloned.1.call-start = ((), (), s32[]{:S(2)}) async-start(), calls=%async_computation.28 | async-start | bytes 1572864 | tf_op jit(solution)/shard_map/psum | solution.py:331
  639.1 107.1 %reduce-scatter.17.cloned.1.call-start = ((), (), s32[]{:S(2)}) async-start(), calls=%async_computation.19 | async-start | bytes 1769472 | tf_op jit(solution)/shard_map/reduce_scatter | solution.py:380
  680.2 134.8 %reduce-scatter.15.cloned.1.call-start = ((), (), s32[]{:S(2)}) async-start(), calls=%async_computation.18 | async-start | bytes 1769472 | tf_op jit(solution)/shard_map/reduce_scatter | solution.py:380
  685.5 193.6 %reduce-scatter.33.cloned.1.call-start = ((), (), s32[]{:S(2)}) async-start(), calls=%async_computation.27 | async-start | bytes 442368
  697.3 247.1 %reduce-scatter.31.cloned.1.call-start = ((), (), s32[]{:S(2)}) async-start(), calls=%async_computation.26 | async-start | bytes 884736
  700.7 46.3 %copy-start.108 = (f32[128,3,64]{0,2,1:T(8,128)S(1)}, f32[128,3,64]{0,2,1:T(8,128)}, u32[]{:S(2)}) copy-start(f32[128,3,64]{0,2,1:T(8,128)} %fusion.8) | copy-start | bytes 294916
  701.8 45.3 %copy-start.115 = (f32[128,32]{0,1:T(8,128)S(1)}, f32[128,32]{0,1:T(8,128)}, u32[]{:S(2)}) copy-start(f32[128,32]{0,1:T(8,128)} %copy-done.114) | copy-start | bytes 49156
  701.8 45.3 %copy-start.117 = (f32[128,32]{0,1:T(8,128)S(1)}, f32[128,32]{0,1:T(8,128)}, u32[]{:S(2)}) copy-start(f32[128,32]{0,1:T(8,128)} %copy-done.116) | copy-start | bytes 49156
  701.8 46.0 %copy-start.30 = (bf16[768,192]{1,0:T(8,128)(2,1)S(1)}, bf16[768,192]{1,0:T(8,128)(2,1)}, u32[]{:S(2)}) copy-start(bf16[768,192]{1,0:T(8,128)(2,1)} %copy-done.29) | copy-start | bytes 884740
  703.0 113.0 %copy-start.111 = (f32[128,32]{0,1:T(8,128)S(1)}, f32[128,32]{0,1:T(8,128)}, u32[]{:S(2)}) copy-start(f32[128,32]{0,1:T(8,128)} %copy-done.110) | copy-start | bytes 49156
  703.0 113.0 %copy-start.113 = (f32[128,32]{0,1:T(8,128)S(1)}, f32[128,32]{0,1:T(8,128)}, u32[]{:S(2)}) copy-start(f32[128,32]{0,1:T(8,128)} %copy-done.112) | copy-start | bytes 49156
  703.0 113.7 %copy-start.38 = (bf16[768,192]{1,0:T(8,128)(2,1)S(1)}, bf16[768,192]{1,0:T(8,128)(2,1)}, u32[]{:S(2)}) copy-start(bf16[768,192]{1,0:T(8,128)(2,1)} %copy-done.37) | copy-start | bytes 884740
  703.0 278.0 %all-reduce.18.cloned.1.call-start = ((), (), s32[]{:S(2)}) async-start(), calls=%async_computation.30 | async-start | bytes 1572864 | tf_op jit(solution)/shard_map/psum | solution.py:288
  748.0 68.9 %copy-start.40 = (bf16[768,192]{1,0:T(8,128)(2,1)S(1)}, bf16[768,192]{1,0:T(8,128)(2,1)}, u32[]{:S(2)}) copy-start(bf16[768,192]{1,0:T(8,128)(2,1)} %copy-done.39) | copy-start | bytes 884740
  819.3 231.4 %reduce-scatter.25.cloned.1.call-start = ((), (), s32[]{:S(2)}) async-start(), calls=%async_computation.23 | async-start | bytes 1769472 | tf_op jit(solution)/shard_map/reduce_scatter | solution.py:439
  821.8 296.7 %reduce-scatter.27.cloned.1.call-start = ((), (), s32[]{:S(2)}) async-start(), calls=%async_computation.24 | async-start | bytes 1769472 | tf_op jit(solution)/shard_map/reduce_scatter | solution.py:440
  824.6 361.9 %reduce-scatter.29.cloned.1.call-start = ((), (), s32[]{:S(2)}) async-start(), calls=%async_computation.25 | async-start | bytes 1769472 | tf_op jit(solution)/shard_map/reduce_scatter | solution.py:441
  827.6 52.9 %copy-start.4 = (bf16[2,128,768]{2,1,0:T(8,128)(2,1)S(1)}, bf16[2,128,768]{2,1,0:T(8,128)(2,1)}, u32[]{:S(2)}) copy-start(bf16[2,128,768]{2,1,0:T(8,128)(2,1)} %param.24) | copy-start | bytes 1179652
  827.6 52.9 %copy-start.96 = (bf16[128,3,64]{0,2,1:T(8,128)(2,1)S(1)}, bf16[128,3,64]{0,2,1:T(8,128)(2,1)}, u32[]{:S(2)}) copy-start(bf16[128,3,64]{0,2,1:T(8,128)(2,1)} %copy-done.95) | copy-start | bytes 147460
  827.6 52.9 %copy-start.135 = (f32[128]{0:T(128)S(1)}, f32[128]{0:T(128)}, u32[]{:S(2)}) copy-start(f32[128]{0:T(128)} %copy-done.134) | copy-start | bytes 1540
  827.6 53.3 %copy-start.106 = (bf16[128,3,64]{0,2,1:T(8,128)(2,1)S(1)}, bf16[128,3,64]{0,2,1:T(8,128)(2,1)}, u32[]{:S(2)}) copy-start(bf16[128,3,64]{0,2,1:T(8,128)(2,1)} %copy-done.105) | copy-start | bytes 147460
  827.6 53.3 %copy-start.145 = (f32[128]{0:T(128)S(1)}, f32[128]{0:T(128)}, u32[]{:S(2)}) copy-start(f32[128]{0:T(128)} %copy-done.144) | copy-start | bytes 1540
  827.6 424.2 %reduce-scatter.19.cloned.1.call-start = ((), (), s32[]{:S(2)}) async-start(), calls=%async_computation.20 | async-start | bytes 884736 | tf_op jit(solution)/shard_map/reduce_scatter | solution.py:434
  882.3 435.2 %reduce-scatter.21.cloned.1.call-start = ((), (), s32[]{:S(2)}) async-start(), calls=%async_computation.21 | async-start | bytes 884736 | tf_op jit(solution)/shard_map/reduce_scatter | solution.py:435
  889.3 493.6 %reduce-scatter.23.cloned.1.call-start = ((), (), s32[]{:S(2)}) async-start(), calls=%async_computation.22 | async-start | bytes 884736 | tf_op jit(solution)/shard_map/reduce_scatter | solution.py:436
  894.6 51.4 %copy-start.104 = (f32[128,384]{0,1:T(8,128)S(1)}, f32[128,384]{0,1:T(8,128)}, u32[]{:S(2)}) copy-start(f32[128,384]{0,1:T(8,128)} %reduce-scatter.15.cloned.1.call-done) | copy-start | bytes 589828
  894.6 51.8 %copy-start.94 = (f32[128,384]{0,1:T(8,128)S(1)}, f32[128,384]{0,1:T(8,128)}, u32[]{:S(2)}) copy-start(f32[128,384]{0,1:T(8,128)} %reduce-scatter.17.cloned.1.call-done) | copy-start | bytes 589828
  1007.5 375.3 %copy-start.1 = (bf16[1,512,768]{2,1,0:T(8,128)(2,1)S(1)}, bf16[1,512,768]{2,1,0:T(8,128)(2,1)}, u32[]{:S(2)}) copy-start(bf16[1,512,768]{2,1,0:T(8,128)(2,1)} %param.41) | copy-start | bytes 2359300
  (159 other events, 1267.8 us)
Sparse Core Ops, SparseCore 0:
  232.2 32.0 all-reduce.15
  639.2 32.5 all-reduce.13
  680.3 65.7 reduce-scatter.16
  750.4 64.5 reduce-scatter.14
  818.7 60.2 reduce-scatter.32
  882.8 61.5 reduce-scatter.30
  947.1 33.8 all-reduce.17
  985.4 65.2 reduce-scatter.24
  1054.7 63.7 reduce-scatter.26
  1122.7 63.7 reduce-scatter.28
  1190.3 61.4 reduce-scatter.18
  1255.9 61.4 reduce-scatter.20
  1321.3 61.4 reduce-scatter.22
where the time goes:
time: 1400 us; the launch traced here: 1390 us
  waiting for transfers between devices  747 us (53%)
  blocking collectives  410 us (29%)
  matrix products  74.7 us (5%)
  local copies, waits for them, and re-layouts  56.4 us (4%)
  other arithmetic  47.4 us (3%)
  starting transfers between devices  35.3 us (3%)
  between operations  18.2 us (1%)
    reduce_scatter x2, waiting for transfers between devices, body(): lax.psum_scatter(key_terms.reshape(tree_rows, 2 * local_width), 'expert',...  110 us
    unnamed x15, waiting for transfers between devices  97.7 us
    reduce_scatter x1, waiting for transfers between devices, body(): lax.psum_scatter(dense_sums[9], 'expert', scatter_dimension=1, tiled=True)  68 us
    reduce_scatter x1, waiting for transfers between devices, body(): lax.psum_scatter(dense_sums[8], 'expert', scatter_dimension=0, tiled=True)  67.8 us
    dot_general x68, matrix products, matmul(): return jnp.dot(left, right, preferred_element_type=jnp.float32)  65.8 us
    reduce_scatter x1, waiting for transfers between devices, body(): lax.psum_scatter(dense_sums[3], 'expert', scatter_dimension=0, tiled=True)  65.6 us
    reduce_scatter x1, waiting for transfers between devices, body(): lax.psum_scatter(dense_sums[2], 'expert', scatter_dimension=0, tiled=True)  65.4 us
    reduce_scatter x1, waiting for transfers between devices, body(): lax.psum_scatter(dense_sums[4], 'expert', scatter_dimension=0, tiled=True)  65.4 us
  transfers between devices with their start and end apart: 21, of which 18 were waited for; matrix products, arithmetic and copies ran while one was open for 8% of the time, Pallas kernels for 0%

commit v1 on v0

--- a/solution.py
+++ b/solution.py
@@ -1,8 +1,11 @@
+import functools
 import math
 
 import jax
 import jax.numpy as jnp
 from jax import lax
+from jax.experimental import pallas as pl
+from jax.experimental.pallas import tpu as pltpu
 from jax.sharding import PartitionSpec as P
 
 HEAD = 64
@@ -110,7 +113,7 @@
     return (weights_exp * (grad_exp - jnp.transpose(delta_rows)[:, :, None])).astype(jnp.bfloat16)
 
 
-def body(
+def plain_body(
     tokens,
     out_grad,
     routes,
@@ -459,6 +462,946 @@
     )
 
 
+MESH = pl.DeviceIdType.MESH
+BF = jnp.bfloat16
+F32 = jnp.float32
+EXACT = lax.Precision.HIGHEST
+VMEM_LIMIT = 62 * 2**20
+
+
+def product(left, right, dims, precision=None):
+    return lax.dot_general(
+        left, right, (dims, ((), ())), preferred_element_type=F32, precision=precision
+    )
+
+
+def dot(left, right, precision=None):
+    return product(left, right, ((1,), (0,)), precision)
+
+
+def dot_nt(left, right, precision=None):
+    return product(left, right, ((1,), (1,)), precision)
+
+
+def dot_tn(left, right, precision=None):
+    return product(left, right, ((0,), (0,)), precision)
+
+
+def iota(shape, dim):
+    return lax.broadcasted_iota(jnp.int32, shape, dim)
+
+
+class Net:
+    def __init__(self, expert_size, send_sems, recv_sems):
+        self.e = lax.axis_index("expert")
+        self.t = lax.axis_index("tensor")
+        self.n = expert_size
+        self.nz = expert_size // 2
+        self.z = self.e // 2
+        self.x = self.e % 2
+        self.core = self.t % 2
+        self.send_sems = send_sems
+        self.recv_sems = recv_sems
+        self.sends = 0
+        self.recvs = 0
+        self.open = []
+
+    def recv_slots(self, count):
+        first = self.recvs
+        self.recvs += count
+        return first
+
+    def ids(self, to):
+        return {"expert": to[0], "tensor": to[1]}
+
+    def push(self, src, dst, to, slot):
+        copy = pltpu.make_async_remote_copy(
+            src_ref=src,
+            dst_ref=dst,
+            send_sem=self.send_sems.at[self.sends],
+            recv_sem=self.recv_sems.at[slot],
+            device_id=self.ids(to),
+            device_id_type=MESH,
+        )
+        self.sends += 1
+        copy.start()
+        self.open.append(copy)
+
+    def landed(self, dst, slot):
+        pltpu.make_async_remote_copy(
+            src_ref=dst,
+            dst_ref=dst,
+            send_sem=self.send_sems.at[0],
+            recv_sem=self.recv_sems.at[slot],
+            device_id=self.ids(self.other_core()),
+            device_id_type=MESH,
+        ).wait_recv()
+
+    def drain_some(self, copies):
+        for copy in copies:
+            copy.wait_send()
+        self.open = [c for c in self.open if not any(c is copy for copy in copies)]
+
+    def drain(self):
+        for copy in self.open:
+            copy.wait_send()
+
+    def other_core(self):
+        return (self.e, self.t + 1 - 2 * self.core)
+
+    def across_y(self):
+        return (self.e, (self.t + 2) % 4)
+
+    def across_x(self):
+        return (self.e + 1 - 2 * self.x, self.t)
+
+    def peer(self, step):
+        return (self.e + step) % self.n
+
+    def greet(self):
+        barrier = pltpu.get_barrier_semaphore()
+        partners = [(self.peer(d), self.t) for d in range(1, self.n)]
+        partners += [self.other_core(), self.across_y()]
+        for to in partners:
+            pl.semaphore_signal(barrier, inc=1, device_id=self.ids(to), device_id_type=MESH)
+        return lambda: pl.semaphore_wait(barrier, len(partners))
+
+
+class Gather:
+    def __init__(self, net, block):
+        self.net, self.block = net, block
+        self.slot = net.recv_slots(net.n)
+
+    def start(self):
+        net = self.net
+        own = self.block(net.e)
+        for d in range(1, net.nz):
+            to = ((net.z + d) % net.nz * 2 + net.x, net.t)
+            net.push(own, own, to, self.slot + net.e)
+        net.push(own, own, net.across_x(), self.slot + net.e)
+
+    def forward(self):
+        net = self.net
+        for d in range(1, net.nz):
+            source = (net.z + d) % net.nz * 2 + net.x
+            part = self.block(source)
+            net.landed(part, self.slot + source)
+            net.push(part, part, net.across_x(), self.slot + source)
+
+    def finish(self):
+        net = self.net
+        for d in range(net.nz):
+            source = (net.z + d) % net.nz * 2 + 1 - net.x
+            net.landed(self.block(source), self.slot + source)
+
+
+class Scatter:
+    def __init__(self, net, block, from_x, from_z):
+        self.net, self.block = net, block
+        self.from_x, self.from_z = from_x, from_z
+        self.slot_x = net.recv_slots(net.nz)
+        self.slot_z = net.recv_slots(net.nz)
+
+    def start(self):
+        net = self.net
+        for d in range(1, net.nz + 1):
+            zz = (net.z + d) % net.nz
+            net.push(
+                self.block(zz * 2 + 1 - net.x), self.from_x.at[zz], net.across_x(), self.slot_x + zz
+            )
+
+    def forward(self):
+        net = self.net
+        for d in range(1, net.nz):
+            zz = (net.z + d) % net.nz
+            net.landed(self.from_x.at[zz], self.slot_x + zz)
+            pair = self.block(zz * 2 + net.x)[...].astype(F32) + self.from_x[zz].astype(F32)
+            self.from_x[zz] = pair.astype(BF)
+            net.push(
+                self.from_x.at[zz],
+                self.from_z.at[net.z],
+                (zz * 2 + net.x, net.t),
+                self.slot_z + net.z,
+            )
+
+    def finish(self):
+        net = self.net
+        net.landed(self.from_x.at[net.z], self.slot_x + net.z)
+        total = self.block(net.e)[...].astype(F32) + self.from_x[net.z].astype(F32)
+        for d in range(1, net.nz):
+            zz = (net.z + d) % net.nz
+            net.landed(self.from_z.at[zz], self.slot_z + zz)
+            total = total + self.from_z[zz].astype(F32)
+        return total
+
+
+class Exchange:
+    def __init__(self, net, outgoing, incoming):
+        self.net, self.outgoing, self.incoming = net, outgoing, incoming
+        self.slot = net.recv_slots(net.n)
+
+    def start(self):
+        net = self.net
+        for d in range(1, net.n):
+            to = net.peer(d)
+            net.push(self.outgoing(to), self.incoming(net.e), (to, net.t), self.slot + net.e)
+
+    def arrive(self, d):
+        source = self.net.peer(d)
+        self.net.landed(self.incoming(source), self.slot + source)
+        return source
+
+
+class CoreSum:
+    def __init__(self, net, out_buf, in_buf):
+        self.net, self.out_buf, self.in_buf = net, out_buf, in_buf
+        self.slot = net.recv_slots(1)
+
+    def start(self, value):
+        self.out_buf[...] = value.astype(self.out_buf.dtype)
+        self.net.push(self.out_buf, self.in_buf, self.net.other_core(), self.slot)
+
+    def finish(self):
+        self.net.landed(self.in_buf, self.slot)
+        return self.in_buf[...].astype(F32)
+
+
+class YSum:
+    def __init__(self, net, out_buf, in_buf):
+        self.net, self.out_buf, self.in_buf = net, out_buf, in_buf
+        self.slot = net.recv_slots(1)
+
+    def start(self, value):
+        self.out_buf[...] = value.astype(self.out_buf.dtype)
+        self.net.push(self.out_buf, self.in_buf, self.net.across_y(), self.slot)
+
+    def finish(self):
+        self.net.landed(self.in_buf, self.slot)
+        return self.out_buf[...].astype(F32) + self.in_buf[...].astype(F32)
+
+
+class CoreShare:
+    def __init__(self, net, halves):
+        self.net, self.halves = net, halves
+        self.slot = net.recv_slots(1)
+
+    def start(self, value):
+        net = self.net
+        self.halves[net.core] = value.astype(self.halves.dtype)
+        part = self.halves.at[net.core]
+        net.push(part, part, net.other_core(), self.slot)
+        self.copy = net.open[-1]
+
+    def finish(self):
+        net = self.net
+        net.landed(self.halves.at[1 - net.core], self.slot)
+        return jnp.concatenate([self.halves[0], self.halves[1]], axis=1)
+
+
+def silu_both(value):
+    gate = jax.nn.sigmoid(value)
+    return value * gate, gate * (1.0 + value * (1.0 - gate))
+
+
+def norm_back(grad_normed, source, scale, gain):
+    weighted = grad_normed * gain
+    inner = jnp.mean(weighted * source, axis=1, keepdims=True)
+    return scale * weighted - scale * scale * scale * source * inner
+
+
+PLACES = ["tok", "cot", "routes", "lengths", "parents", "wq", "wk", "wv", "wo", "ext"]
+PLACES += ["sg", "su", "sd", "eg", "eu", "ed"]
+PLACES += ["out", "gtok", "dqkv", "dwo", "dext", "dshared", "dgains", "deg", "deu", "ded"]
+
+
+def scratch_shapes(s):
+    n, rows, width, half = s["n"], s["rows"], s["width"], s["half"]
+    depth, hidden, shared, slots = s["depth"], s["hidden"], s["shared"], s["slots"]
+    micro, local, heads, nz = s["micro"], s["local"], s["heads"], s["n"] // 2
+    tree = n * local
+    vm = pltpu.VMEM
+    return dict(
+        w_small=vm((3, n, depth, width), BF),
+        w_o=vm((n, depth, width), BF),
+        w_ext=vm((n, depth, 128), BF),
+        w_sh=vm((3, n, depth, shared), BF),
+        pairs=vm((2, micro, n, local, width), BF),
+        q_rows=vm((micro, heads * local, width), BF),
+        expo=vm((micro, heads * local, tree), F32),
+        mixed=vm((rows, width), F32),
+        choice=vm((rows, n * slots), BF),
+        res=vm((rows, 2 * half), F32),
+        n_one=vm((rows, 2 * half), BF),
+        n_two=vm((2, rows, half), BF),
+        mixed_low=vm((rows, width), BF),
+        c_out=vm((n, slots, half), BF),
+        c_in=vm((2, n, slots, half), BF),
+        h_out=vm((n, 8, slots), F32),
+        h_in=vm((n, 8, slots), F32),
+        x_out=vm((n, slots, half), BF),
+        x_in=vm((2, n, slots, half), BF),
+        gate_col=vm((n, slots, 1), F32),
+        e_h=vm((n * slots, hidden), BF),
+        e_dg=vm((n * slots, hidden), BF),
+        e_du=vm((n * slots, hidden), BF),
+        y_part=vm((2, n, slots, half), BF),
+        g_part=vm((2, n, slots, half), BF),
+        y_core=vm((n, slots, half), BF),
+        g_core=vm((n, slots, half), BF),
+        y_out=vm((n, slots, half), BF),
+        g_out=vm((n, slots, half), BF),
+        y_in=vm((n, slots, half), BF),
+        g_in=vm((n, slots, half), BF),
+        d_out=vm((n, 8, slots), F32),
+        d_in=vm((n, 8, slots), F32),
+        d_tensor=vm((4, 8, slots), F32),
+        core_buf=vm((4, rows, half), F32),
+        core_low=vm((4, rows, half), BF),
+        y_buf=vm((8, rows, half), BF),
+        share=vm((2, 2, rows, half), F32),
+        share_low=vm((2, rows, half), BF),
+        kv_part=vm((micro, 2, n, local, width), BF),
+        kv_fx=vm((micro, nz, 2, local, width), BF),
+        kv_fz=vm((micro, nz, 2, local, width), BF),
+        sh_part=vm((3, n, depth, shared), BF),
+        sh_fx=vm((nz, 3, depth, shared), BF),
+        sh_fz=vm((nz, 3, depth, shared), BF),
+        o_part=vm((2, n, depth, width), BF),
+        o_fx=vm((nz, 2, depth, width), BF),
+        o_fz=vm((nz, 2, depth, width), BF),
+        kvw_part=vm((2, n, depth, width), BF),
+        kvw_fx=vm((nz, 2, depth, width), BF),
+        kvw_fz=vm((nz, 2, depth, width), BF),
+        ext_part=vm((n, depth, 128), BF),
+        ext_fx=vm((nz, depth, 128), BF),
+        ext_fz=vm((nz, depth, 128), BF),
+        gains_out=vm((n, 8, 128), F32),
+        gains_in=vm((n, 8, 128), F32),
+        stage=vm((2, half, hidden), F32),
+        stage_d=vm((hidden, half), F32),
+        save_sems=pltpu.SemaphoreType.DMA((6,)),
+        send_sems=pltpu.SemaphoreType.DMA((180,)),
+        recv_sems=pltpu.SemaphoreType.DMA((200,)),
+    )
+
+
+def layer_kernel(s, names, *refs):
+    r = dict(zip(names, refs))
+    n, rows, width, half = s["n"], s["rows"], s["width"], s["half"]
+    depth, hidden, shared, slots = s["depth"], s["hidden"], s["shared"], s["slots"]
+    micro, local, heads = s["micro"], s["local"], s["heads"]
+    model, tree, cap = 2 * half, n * local, slots // micro
+    experts = s["experts"]
+    net = Net(n, r["send_sems"], r["recv_sems"])
+    me, core = net.e, net.core
+    ready = net.greet()
+    my_half = pl.ds(pl.multiple_of(core * half, 128), half)
+
+    for i, name in enumerate(("wq", "wk", "wv")):
+        r["w_small"][i, me] = r[name][...]
+    r["w_o"][me] = r["wo"][...]
+    r["w_ext"][me] = r["ext"][...]
+    for i, name in enumerate(("sg", "su", "sd")):
+        r["w_sh"][i, me] = r[name][...]
+    get_small = Gather(net, lambda b: r["w_small"].at[:, b])
+    get_ext = Gather(net, lambda b: r["w_ext"].at[b])
+    get_o = Gather(net, lambda b: r["w_o"].at[b])
+    get_sh = [Gather(net, lambda b, i=i: r["w_sh"].at[i, b]) for i in range(3)]
+    get_pairs = Gather(net, lambda b: r["pairs"].at[:, :, b])
+    ready()
+    get_small.start()
+    get_ext.start()
+
+    lane = iota((rows, 128), 1) - 8
+    hot_one = lane == r["routes"][:, 0:1]
+    hot_two = lane == r["routes"][:, 1:2]
+    hits = (hot_one | hot_two).astype(F32)
+    row_a, row_b = iota((rows, rows), 0), iota((rows, rows), 1)
+    earlier = ((row_b < row_a) & (row_a // local == row_b // local)).astype(BF)
+    rank = dot(earlier, hits.astype(BF))
+    rank = jnp.where(hits > 0.5, rank, -1.0)
+    spread = (iota((128, n * slots), 0) - 8 == iota((128, n * slots), 1) // slots).astype(BF)
+    rank_wide = dot(rank.astype(BF), spread)
+    column = iota((rows, n * slots), 1) % slots
+    same_micro = column // cap == iota((rows, n * slots), 0) // local
+    taken = (rank_wide == (column % cap).astype(F32)) & same_micro
+    r["choice"][...] = taken.astype(BF)
+
+    send_c = Exchange(net, lambda b: r["c_out"].at[b], lambda b: r["c_in"].at[core, b])
+    send_h = Exchange(net, lambda b: r["h_out"].at[b], lambda b: r["h_in"].at[b])
+    picked = dot_tn(r["choice"][...], r["cot"][:, my_half]).astype(BF).reshape(n, slots, half)
+    r["c_out"][...] = picked
+    r["c_in"][core, me] = r["c_out"][me]
+    hit_rows = dot_tn(hits.astype(BF), r["choice"][...])[8:16]
+    for b in range(n):
+        r["h_out"][b] = hit_rows[:, b * slots : (b + 1) * slots]
+    r["h_in"][me] = r["h_out"][me]
+
+    def segments(m):
+        starts, ends, paths, shifts, begin = [], [], [], [], 0
+        for seg in range(s["segs"]):
+            size = r["lengths"][m, seg]
+            starts.append(begin)
+            ends.append(begin + size)
+            begin = begin + size
+            if seg == 0:
+                paths.append(jnp.int32(1))
+                shifts.append(jnp.int32(0))
+            else:
+                parent = r["parents"][m, seg]
+                path, shift = jnp.int32(0), jnp.int32(0)
+                for other in range(seg):
+                    is_parent = parent == other
+                    path = jnp.where(is_parent, paths[other], path)
+                    shift = jnp.where(
+                        is_parent, shifts[other] + ends[other] - starts[other], shift
+                    )
+                paths.append(path + (1 << seg))
+                shifts.append(shift)
+        return starts, ends, paths, shifts
+
+    tables = [segments(m) for m in range(micro)]
+
+    def row_values(m, ids):
+        starts, ends, paths, shifts = tables[m]
+        path, place, own = jnp.zeros_like(ids), jnp.zeros_like(ids), jnp.zeros_like(ids)
+        for seg in range(s["segs"]):
+            inside = (ids >= starts[seg]) & (ids < ends[seg])
+            path = jnp.where(inside, paths[seg], path)
+            place = jnp.where(inside, ids - starts[seg] + shifts[seg], place)
+            own = jnp.where(inside, 1 << seg, own)
+        return path, place, own
+
+    place = jnp.concatenate(
+        [row_values(m, me * local + iota((local, 1), 0))[1] for m in range(micro)], axis=0
+    )
+    turn = iota((1, width), 1) % 32
+    frequency = jnp.exp(turn.astype(F32) * (-math.log(ROPE_BASE) / 32.0))
+    angle = place.astype(F32) * frequency
+    cosine, sine = jnp.cos(angle), jnp.sin(angle)
+    swap_r, swap_c = iota((width, width), 0), iota((width, width), 1)
+    lower = swap_c % HEAD < HEAD // 2
+    swap = jnp.where(lower & (swap_r == swap_c + HEAD // 2), -1.0, 0.0)
+    swap = jnp.where(~lower & (swap_r == swap_c - HEAD // 2), 1.0, swap)
+    swap_low = swap.astype(BF)
+
+    tok = r["tok"][...].astype(F32)
+    scale_one = lax.rsqrt(jnp.mean(tok * tok, axis=1, keepdims=True) + EPSILON)
+
+    get_small.forward()
+    get_ext.forward()
+    get_ext.finish()
+    ext_all = r["w_ext"][...].reshape(model, 128)
+    ext_turned = ext_all.astype(F32).T
+    gain_one, gain_two = ext_turned[0:1], ext_turned[1:2]
+    r["n_one"][...] = (tok * scale_one * gain_one).astype(BF)
+    get_small.finish()
+
+    def small(i):
+        return r["w_small"][i].reshape(model, width)
+
+    def turned(weight):
+        normed = r["n_one"][...]
+        plain = dot(normed, weight)
+        swapped = dot(normed, dot(weight, swap_low).astype(BF))
+        return (plain * cosine + swapped * sine).astype(BF)
+
+    keys = turned(small(1)).reshape(micro, local, width)
+    values = dot(r["n_one"][...], small(2)).astype(BF).reshape(micro, local, width)
+    for m in range(micro):
+        r["pairs"][0, m, me] = keys[m]
+        r["pairs"][1, m, me] = values[m]
+    get_pairs.start()
+    get_o.start()
+    queries = turned(small(0)).reshape(micro, local, width)
+    head_of = iota((1, width), 1) // HEAD
+    head_masks = [head_of == h for h in range(heads)]
+
+    def by_head(block):
+        return jnp.concatenate(
+            [jnp.where(mask, block, jnp.zeros_like(block)) for mask in head_masks], axis=0
+        )
+
+    def join_heads(stack):
+        total = jnp.zeros((local, width), F32)
+        for h, mask in enumerate(head_masks):
+            total = total + jnp.where(mask, stack[h * local : (h + 1) * local], 0.0)
+        return total
+
+    for m in range(micro):
+        r["q_rows"][m] = by_head(queries[m])
+    get_pairs.forward()
+    send_c.start()
+    send_h.start()
+    for g in get_sh:
+        g.start()
+    get_pairs.finish()
+    score_scale = HEAD**-0.5
+    totals = []
+    for m in range(micro):
+        key_rows = r["pairs"][0, m].reshape(tree, width)
+        value_rows = r["pairs"][1, m].reshape(tree, width)
+        ids = me * local + iota((heads * local, 1), 0) % local
+        path, unused, unused_two = row_values(m, ids)
+        key_ids = iota((1, tree), 1)
+        unused, unused_two, key_seg = row_values(m, key_ids)
+        seen = ((path & key_seg) != 0) & (key_ids <= ids)
+        scores = dot_nt(r["q_rows"][m], key_rows) * score_scale
+        expo = jnp.where(seen, jnp.exp(scores), 0.0)
+        r["expo"][m] = expo
+        total = jnp.sum(expo, axis=1, keepdims=True)
+        totals.append(total)
+        mixed = join_heads(dot(expo.astype(BF), value_rows) / total)
+        r["mixed"][m * local : (m + 1) * local] = mixed
+    r["mixed_low"][...] = r["mixed"][...].astype(BF)
+    get_o.forward()
+    get_o.finish()
+
+    def o_half(h):
+        return r["w_o"][pl.ds(h * (n // 2), n // 2)].reshape(half, width)
+
+    core_bufs = [r["core_buf"].at[i] for i in range(4)]
+    core_bufs[2:2] = [r["core_low"].at[i] for i in range(4)]
+    core_sum = [CoreSum(net, core_bufs[2 * i], core_bufs[2 * i + 1]) for i in range(4)]
+    y_sum = [YSum(net, r["y_buf"].at[2 * i], r["y_buf"].at[2 * i + 1]) for i in range(4)]
+    share = [CoreShare(net, r["share"].at[i]) for i in (0, 1, 0)]
+
+    core_sum[0].start(dot_nt(r["mixed_low"][...], o_half(1 - core)))
+    mine = dot_nt(r["mixed_low"][...], o_half(core))
+    y_sum[0].start(mine + core_sum[0].finish())
+    slot_c = net.recv_slots(n)
+    slot_x = net.recv_slots(n)
+
+    def hand_over(buf, source, slot):
+        part = buf.at[core, source]
+        net.push(part, part, net.other_core(), slot + source)
+
+    def take_over(buf, slot):
+        for b in range(n):
+            net.landed(buf.at[1 - core, b], slot + b)
+
+    handed_c = len(net.open)
+    hand_over(r["c_in"], me, slot_c)
+    for d in range(1, n):
+        hand_over(r["c_in"], send_c.arrive(d), slot_c)
+    handed_c = net.open[handed_c:]
+    share[0].start(y_sum[0].finish())
+    res = tok + share[0].finish()
+    r["res"][...] = res
+    scale_two = lax.rsqrt(jnp.mean(res * res, axis=1, keepdims=True) + EPSILON)
+    normed_two = (res * scale_two * gain_two).astype(BF)
+    for h in range(2):
+        r["n_two"][h] = normed_two[:, h * half : (h + 1) * half]
+
+    send_x = Exchange(net, lambda b: r["x_out"].at[b], lambda b: r["x_in"].at[core, b])
+    r["x_out"][...] = (
+        dot_tn(r["choice"][...], r["n_two"][core]).astype(BF).reshape(n, slots, half)
+    )
+    send_x.start()
+    r["x_in"][core, me] = r["x_out"][me]
+    hand_over(r["x_in"], me, slot_x)
+
+    logits = dot(normed_two, ext_all)
+    z_one = jnp.sum(jnp.where(hot_one, logits, 0.0), axis=1, keepdims=True)
+    z_two = jnp.sum(jnp.where(hot_two, logits, 0.0), axis=1, keepdims=True)
+    z_top = jnp.maximum(z_one, z_two)
+    e_one, e_two = jnp.exp(z_one - z_top), jnp.exp(z_two - z_top)
+    gates = jnp.where(hot_one, e_one, jnp.where(hot_two, e_two, 0.0)) / (e_one + e_two)
+
+    for g in get_sh:
+        g.forward()
+    for g in get_sh:
+        g.finish()
+
+    def wide(i):
+        return r["w_sh"][i].reshape(model, shared)
+
+    def wide_half(i, h):
+        return r["w_sh"][i, pl.ds(h * (n // 2), n // 2)].reshape(half, shared)
+
+    shared_g = dot(normed_two, wide(0))
+    shared_u = dot(normed_two, wide(1))
+    act, slope = silu_both(shared_g)
+    shared_h = (act * shared_u).astype(BF)
+    grad_h = dot(r["cot"][...], wide(2))
+    grad_g = (grad_h * shared_u * slope).astype(BF)
+    grad_u = (grad_h * act).astype(BF)
+    core_sum[1].start(dot_nt(grad_g, wide_half(0, 1 - core)) + dot_nt(grad_u, wide_half(1, 1 - core)))
+    core_sum[2].start(dot_nt(shared_h, wide_half(2, 1 - core)))
+    shared_grad = dot_nt(grad_g, wide_half(0, core)) + dot_nt(grad_u, wide_half(1, core))
+    shared_y = dot_nt(shared_h, wide_half(2, core))
+    r["sh_part"][0] = dot_tn(normed_two, grad_g).astype(BF).reshape(n, depth, shared)
+    r["sh_part"][1] = dot_tn(normed_two, grad_u).astype(BF).reshape(n, depth, shared)
+    r["sh_part"][2] = dot_tn(r["cot"][...], shared_h).astype(BF).reshape(n, depth, shared)
+    sum_sh = Scatter(net, lambda b: r["sh_part"].at[:, b], r["sh_fx"], r["sh_fz"])
+
+    for d in range(1, n):
+        hand_over(r["x_in"], send_x.arrive(d), slot_x)
+    for d in range(1, n):
+        send_h.arrive(d)
+    take_over(r["c_in"], slot_c)
+    take_over(r["x_in"], slot_x)
+    net.drain_some(handed_c)
+    ext_low = ext_turned.astype(BF)
+    z_all = dot_nt(ext_low[:, :half], r["x_in"][0].reshape(n * slots, half))
+    z_all = (z_all + dot_nt(ext_low[:, half:], r["x_in"][1].reshape(n * slots, half)))[8:16]
+    hit_all = jnp.concatenate([r["h_in"][b] for b in range(n)], axis=1)
+    own_row = iota((8, n * slots), 0) == me
+    z_own = jnp.sum(jnp.where(own_row, z_all, 0.0), axis=0, keepdims=True)
+    z_other = jnp.sum(jnp.where(own_row, 0.0, z_all * hit_all), axis=0, keepdims=True)
+    z_top = jnp.maximum(z_own, z_other)
+    e_own, e_other = jnp.exp(z_own - z_top), jnp.exp(z_other - z_top)
+    gate_row = e_own / (e_own + e_other)
+    eye = iota((slots, slots), 0) == iota((slots, slots), 1)
+    for b in range(n):
+        part = jnp.where(eye, gate_row[:, b * slots : (b + 1) * slots], 0.0)
+        r["gate_col"][b] = jnp.sum(part, axis=1, keepdims=True)
+
+    group = 2
+
+    def expert_step(i, carry):
+        span = pl.ds(i * group, group)
+        flat = pl.ds(pl.multiple_of(i * group * slots, group * slots), group * slots)
+        count = group * slots
+        x_half = [r["x_in"][h, span].reshape(count, half) for h in range(2)]
+        c_half = [r["c_in"][h, span].reshape(count, half) for h in range(2)]
+        gate = r["gate_col"][span].reshape(count, 1)
+        cut = [slice(0, half), slice(half, model)]
+        gate_pre = dot(x_half[0], r["eg"][cut[0]]) + dot(x_half[1], r["eg"][cut[1]])
+        up_pre = dot(x_half[0], r["eu"][cut[0]]) + dot(x_half[1], r["eu"][cut[1]])
+        act, slope = silu_both(gate_pre)
+        hid = (act * up_pre).astype(BF)
+        grad_y = [(gate * c.astype(F32)).astype(BF) for c in c_half]
+        grad_hid = dot_nt(grad_y[0], r["ed"][:, cut[0]]) + dot_nt(grad_y[1], r["ed"][:, cut[1]])
+        grad_g = (grad_hid * up_pre * slope).astype(BF)
+        grad_u = (grad_hid * act).astype(BF)
+        r["e_h"][flat] = hid
+        r["e_dg"][flat] = grad_g
+        r["e_du"][flat] = grad_u
+        dots = jnp.zeros((count, 1), F32)
+        for h in range(2):
+            y = dot(hid, r["ed"][:, cut[h]])
+            r["y_part"][h, span] = y.astype(BF).reshape(group, slots, half)
+            dots = dots + jnp.sum(y * c_half[h].astype(F32), axis=1, keepdims=True)
+            back = dot_nt(grad_g, r["eg"][cut[h]]) + dot_nt(grad_u, r["eu"][cut[h]])
+            r["g_part"][h, span] = back.astype(BF).reshape(group, slots, half)
+            r["c_in"][h, span] = grad_y[h].reshape(group, slots, half)
+        for b in range(group):
+            part = jnp.where(eye, dots[b * slots : (b + 1) * slots], 0.0)
+            line = jnp.sum(part, axis=0, keepdims=True)
+            r["d_out"][i * group + b] = jnp.broadcast_to(line, (8, slots))
+        return carry
+
+    lax.fori_loop(0, n // group, expert_step, 0)
+
+    send_g = Exchange(net, lambda b: r["g_out"].at[b], lambda b: r["g_in"].at[b])
+    send_y = Exchange(net, lambda b: r["y_out"].at[b], lambda b: r["y_in"].at[b])
+    send_d = Exchange(net, lambda b: r["d_out"].at[b], lambda b: r["d_in"].at[b])
+    slot_gc, slot_yc = net.recv_slots(1), net.recv_slots(1)
+    net.push(r["g_part"].at[1 - core], r["g_core"], net.other_core(), slot_gc)
+    net.push(r["y_part"].at[1 - core], r["y_core"], net.other_core(), slot_yc)
+    send_d.start()
+    r["d_in"][me] = r["d_out"][me]
+    net.landed(r["g_core"], slot_gc)
+    r["g_out"][...] = (r["g_part"][core].astype(F32) + r["g_core"][...].astype(F32)).astype(BF)
+    send_g.start()
+    r["g_in"][me] = r["g_out"][me]
+    net.landed(r["y_core"], slot_yc)
+    r["y_out"][...] = (r["y_part"][core].astype(F32) + r["y_core"][...].astype(F32)).astype(BF)
+    send_y.start()
+    r["y_in"][me] = r["y_out"][me]
+    sum_sh.start()
+
+    dg_all, du_all = r["e_dg"], r["e_du"]
+    saves = []
+    for h in range(2):
+        cut = slice(h * half, (h + 1) * half)
+        rows_x = r["x_in"][h].reshape(n * slots, half)
+        for i, (target, grads) in enumerate((("deg", dg_all), ("deu", du_all))):
+            if h == 1:
+                saves[i].wait()
+            r["stage"][i] = dot_tn(rows_x, grads[...])
+            save = pltpu.make_async_copy(r["stage"].at[i], r[target].at[cut], r["save_sems"].at[2 * h + i])
+            save.start()
+            saves.append(save)
+        if h == 1:
+            saves[2].wait()
+        r["stage_d"][...] = dot_tn(r["e_h"][...], r["c_in"][h].reshape(n * slots, half))
+        save = pltpu.make_async_copy(r["stage_d"], r["ded"].at[:, cut], r["save_sems"].at[4 + h])
+        save.start()
+        saves.append(save)
+
+    for d in range(1, n):
+        send_d.arrive(d)
+    eight = iota((8, slots), 0)
+    d_rows = jnp.zeros((8, slots), F32)
+    for b in range(n):
+        d_rows = d_rows + jnp.where(eight == b, r["d_in"][b], 0.0)
+    d_core = CoreSum(net, r["d_tensor"].at[0], r["d_tensor"].at[1])
+    d_y = YSum(net, r["d_tensor"].at[2], r["d_tensor"].at[3])
+    d_core.start(d_rows)
+    d_y.start(d_rows + d_core.finish())
+
+    for d in range(1, n):
+        send_g.arrive(d)
+    moe_grad = dot(r["choice"][...], r["g_in"][...].reshape(n * slots, half))
+    y_sum[1].start(moe_grad + shared_grad + core_sum[1].finish())
+    d_rows = d_y.finish()
+    grad_gate = jnp.zeros((rows, 128), F32)
+    for b in range(n):
+        cut = slice(b * slots, (b + 1) * slots)
+        part = r["choice"][:, cut].astype(F32) * d_rows[b : b + 1]
+        grad_gate = jnp.where(lane == b, jnp.sum(part, axis=1, keepdims=True), grad_gate)
+    inner = jnp.sum(gates * grad_gate, axis=1, keepdims=True)
+    grad_logits = (gates * (grad_gate - inner)).astype(BF)
+    share[1].start(y_sum[1].finish())
+    grad_two = share[1].finish() + dot_nt(grad_logits, ext_all)
+    res = r["res"][...]
+    cot = r["cot"][...].astype(F32)
+    grad_res = cot + norm_back(grad_two, res, scale_two, gain_two)
+    gain_two_row = jnp.sum(grad_two * res * scale_two, axis=0, keepdims=True)
+    r["ext_part"][...] = dot_tn(normed_two, grad_logits).astype(BF).reshape(n, depth, 128)
+    sum_ext = Scatter(net, lambda b: r["ext_part"].at[b], r["ext_fx"], r["ext_fz"])
+    sum_ext.start()
+    grad_attn = grad_res.astype(BF)
+
+    o_all = r["w_o"][...].reshape(model, width)
+    grad_mixed = dot(grad_attn, o_all)
+    kv_sums = []
+    grad_queries = []
+    for m in range(micro):
+        cut = slice(m * local, (m + 1) * local)
+        key_rows = r["pairs"][0, m].reshape(tree, width)
+        value_rows = r["pairs"][1, m].reshape(tree, width)
+        gm = by_head(grad_mixed[cut])
+        mixed3 = jnp.concatenate([r["mixed"][cut]] * heads, axis=0)
+        delta = jnp.sum(gm * mixed3, axis=1, keepdims=True) / totals[m]
+        grad_summed = (gm / totals[m]).astype(BF)
+        expo = r["expo"][m]
+        ds = (expo * (dot_nt(grad_summed, value_rows) - delta)).astype(BF)
+        grad_k = dot_tn(ds, r["q_rows"][m]) * score_scale
+        grad_v = dot_tn(expo.astype(BF), grad_summed)
+        r["kv_part"][m, 0] = grad_k.astype(BF).reshape(n, local, width)
+        r["kv_part"][m, 1] = grad_v.astype(BF).reshape(n, local, width)
+        kv = Scatter(
+            net,
+            lambda b, m=m: r["kv_part"].at[m, :, b],
+            r["kv_fx"].at[m],
+            r["kv_fz"].at[m],
+        )
+        kv.start()
+        kv_sums.append(kv)
+        grad_queries.append(join_heads(dot(ds, key_rows)) * score_scale)
+
+    def turned_back(grad):
+        return (grad * cosine - dot(grad, swap, EXACT) * sine).astype(BF)
+
+    grad_q = turned_back(jnp.concatenate(grad_queries, axis=0))
+    r["o_part"][0] = dot_tn(grad_attn, r["mixed_low"][...]).astype(BF).reshape(n, depth, width)
+    r["o_part"][1] = dot_tn(r["n_one"][...], grad_q).astype(BF).reshape(n, depth, width)
+    sum_o = Scatter(net, lambda b: r["o_part"].at[:, b], r["o_fx"], r["o_fz"])
+    for kv in kv_sums:
+        kv.forward()
+    sum_o.start()
+    sum_sh.forward()
+    sum_ext.forward()
+
+    for d in range(1, n):
+        send_y.arrive(d)
+    moe_y = jnp.zeros((rows, half), F32)
+    weighed_hi, weighed_lo = [], []
+    for b in range(n):
+        gate = jnp.sum(jnp.where(lane == b, gates, 0.0), axis=1, keepdims=True)
+        gate_hi = gate.astype(BF).astype(F32)
+        pick = r["choice"][:, b * slots : (b + 1) * slots].astype(F32)
+        weighed_hi.append((pick * gate_hi).astype(BF))
+        weighed_lo.append((pick * (gate - gate_hi)).astype(BF))
+    y_rows = r["y_in"][...].reshape(n * slots, half)
+    moe_y = dot(jnp.concatenate(weighed_hi, axis=1), y_rows)
+    moe_y = moe_y + dot(jnp.concatenate(weighed_lo, axis=1), y_rows)
+    y_sum[2].start(moe_y + shared_y + core_sum[2].finish())
+
+    sums = [kv.finish() for kv in kv_sums]
+    grad_k = turned_back(jnp.concatenate([p[0] for p in sums], axis=0))
+    grad_v = jnp.concatenate([p[1] for p in sums], axis=0).astype(BF)
+
+    def small_half(i, h):
+        return r["w_small"][i, pl.ds(h * (n // 2), n // 2)].reshape(half, width)
+
+    def grad_one_half(h):
+        total = dot_nt(grad_q, small_half(0, h)) + dot_nt(grad_k, small_half(1, h))
+        return total + dot_nt(grad_v, small_half(2, h))
+
+    core_sum[3].start(grad_one_half(1 - core))
+    mine = grad_one_half(core)
+    y_sum[3].start(mine + core_sum[3].finish())
+    r["kvw_part"][0] = dot_tn(r["n_one"][...], grad_k).astype(BF).reshape(n, depth, width)
+    r["kvw_part"][1] = dot_tn(r["n_one"][...], grad_v).astype(BF).reshape(n, depth, width)
+    sum_kvw = Scatter(
+        net, lambda b: r["kvw_part"].at[:, b], r["kvw_fx"], r["kvw_fz"]
+    )
+    sum_kvw.start()
+    net.drain_some([share[0].copy])
+    share[2].start(y_sum[3].finish())
+    share_out = CoreShare(net, r["share_low"])
+    res_half = jnp.where(core == 0, r["res"][:, :half], r["res"][:, half:])
+    share_out.start(res_half + y_sum[2].finish())
+    sum_o.forward()
+    sum_kvw.forward()
+
+    grad_one = share[2].finish()
+    tok = r["tok"][...].astype(F32)
+    r["gtok"][...] = grad_res + norm_back(grad_one, tok, scale_one, gain_one)
+    gain_one_row = jnp.sum(grad_one * tok * scale_one, axis=0, keepdims=True)
+    block_of = iota((n, model), 0) == iota((n, model), 1) // depth
+    to_lane = (iota((model, 128), 0) % depth == iota((model, 128), 1)).astype(F32)
+    first = dot(jnp.where(block_of, gain_one_row, 0.0), to_lane, EXACT)
+    second = dot(jnp.where(block_of, gain_two_row, 0.0), to_lane, EXACT)
+    for b in range(n):
+        both = jnp.where(iota((8, 128), 0) == 0, first[b : b + 1], second[b : b + 1])
+        r["gains_out"][b] = both
+    send_gains = Exchange(net, lambda b: r["gains_out"].at[b], lambda b: r["gains_in"].at[b])
+    send_gains.start()
+    r["gains_in"][me] = r["gains_out"][me]
+    r["out"][...] = share_out.finish()
+
+    sum_sh_total = sum_sh.finish()
+    r["dshared"][...] = sum_sh_total
+    r["dext"][...] = sum_ext.finish()
+    o_total = sum_o.finish()
+    r["dwo"][...] = o_total[0]
+    r["dqkv"][0] = o_total[1]
+    kvw_total = sum_kvw.finish()
+    r["dqkv"][1] = kvw_total[0]
+    r["dqkv"][2] = kvw_total[1]
+    gains = jnp.zeros((8, 128), F32)
+    for d in range(1, n):
+        send_gains.arrive(d)
+    for b in range(n):
+        gains = gains + r["gains_in"][b]
+    r["dgains"][...] = gains
+    for save in saves[3:]:
+        save.wait()
+    net.drain()
+
+
+def fits(mesh):
+    return mesh.shape["expert"] == 8 and mesh.shape["tensor"] == 4
+
+
+def fused_body(
+    tokens,
+    out_grad,
+    routes,
+    lengths,
+    parents,
+    attn_gain,
+    ffn_gain,
+    w_query,
+    w_key,
+    w_value,
+    w_out,
+    router,
+    shared_gate,
+    shared_up,
+    shared_down,
+    expert_gate,
+    expert_up,
+    expert_down,
+):
+    micro, local, model = tokens.shape
+    n = lax.axis_size("expert")
+    experts = router.shape[1]
+    depth, width = w_query.shape
+    cap = 4 * local // experts
+    hidden, shared = expert_gate.shape[2], shared_gate.shape[1]
+    s = dict(
+        n=n,
+        micro=micro,
+        local=local,
+        rows=micro * local,
+        half=model // 2,
+        depth=depth,
+        width=width,
+        heads=width // HEAD,
+        hidden=hidden,
+        shared=shared,
+        slots=micro * cap,
+        experts=experts,
+        segs=lengths.shape[1],
+    )
+    rows = micro * local
+    ext = jnp.concatenate(
+        [
+            attn_gain[:, None],
+            ffn_gain[:, None],
+            jnp.zeros((depth, 6), BF),
+            router,
+            jnp.zeros((depth, 120 - experts), BF),
+        ],
+        axis=1,
+    )
+    scratch = scratch_shapes(s)
+    names = PLACES + list(scratch)
+    shape = jax.ShapeDtypeStruct
+    vmem, smem = pl.BlockSpec(memory_space=pltpu.VMEM), pl.BlockSpec(memory_space=pltpu.SMEM)
+    out, gtok, dqkv, dwo, dext, dshared, dgains, deg, deu, ded = pl.pallas_call(
+        functools.partial(layer_kernel, s, names),
+        out_shape=(
+            shape((rows, model), BF),
+            shape((rows, model), F32),
+            shape((3, depth, width), F32),
+            shape((depth, width), F32),
+            shape((depth, 128), F32),
+            shape((3, depth, shared), F32),
+            shape((8, 128), F32),
+            shape((model, hidden), F32),
+            shape((model, hidden), F32),
+            shape((hidden, model), F32),
+        ),
+        in_specs=[vmem] * 3 + [smem] * 2 + [vmem] * 11,
+        out_specs=[vmem] * 7 + [pl.BlockSpec(memory_space=pl.ANY)] * 3,
+        scratch_shapes=list(scratch.values()),
+        compiler_params=pltpu.CompilerParams(
+            collective_id=0, has_side_effects=True, vmem_limit_bytes=VMEM_LIMIT
+        ),
+    )(
+        tokens.reshape(rows, model),
+        out_grad.reshape(rows, model),
+        routes.reshape(rows, 2),
+        lengths,
+        parents,
+        w_query,
+        w_key,
+        w_value,
+        w_out.T,
+        ext,
+        shared_gate,
+        shared_up,
+        shared_down.T,
+        expert_gate[0],
+        expert_up[0],
+        expert_down[0],
+    )
+    return (
+        out.reshape(micro, local, model),
+        gtok.reshape(micro, local, model),
+        dgains[0, :depth],
+        dgains[1, :depth],
+        dqkv[0],
+        dqkv[1],
+        dqkv[2],
+        dwo.T,
+        dext[:, 8 : 8 + experts],
+        dshared[0],
+        dshared[1],
+        dshared[2].T,
+        deg[None],
+        deu[None],
+        ded[None],
+    )
+
+
 def solution(mesh):
     in_specs = (
         P(None, "expert", None),
@@ -497,4 +1440,5 @@
         P("expert", None, "tensor"),
         P("expert", "tensor", None),
     )
-    return jax.shard_map(body, mesh=mesh, in_specs=in_specs, out_specs=out_specs, check_vma=False)
+    chosen = fused_body if fits(mesh) else plain_body
+    return jax.shard_map(chosen, mesh=mesh, in_specs=in_specs, out_specs=out_specs, check_vma=False)

time: 1400 us -> 291 us (0.21)
  waiting for transfers between devices: 747 us -> 0 us
  blocking collectives: 410 us -> 0 us
  Pallas kernels: 0 us -> 269 us
  matrix products: 74.7 us -> 0 us
  other arithmetic: 47.4 us -> 0 us
  local copies, waits for them, and re-layouts: 56.4 us -> 21 us
  starting transfers between devices: 35.3 us -> 0 us
  between operations: 18.2 us -> 0.69 us
    reduce_scatter x8 -> x0, waiting for transfers between devices: 484 us -> none  [the longest x2 110 us: body(): lax.psum_scatter(key_terms.reshape(tree_rows, 2 * local_width), 'expert',...]
    all_gather x10 -> x0, blocking collectives: 361 us -> none  [the longest x1 59.4 us: body(): lax.all_gather(shared_gate, 'expert', axis=0, tiled=True)]
    pallas_call x0 -> x1, Pallas kernels: none -> 269 us  [fused_body(): pl.pallas_call(functools.partial(layer_kernel, s, names), out_shape=(shap...]
    unnamed x15 -> x0, waiting for transfers between devices: 97.7 us -> none
    psum x3 -> x0, waiting for transfers between devices: 94.4 us -> none  [the longest x1 33.3 us: body(): lax.psum((shared_y + moe_part).astype(jnp.bfloat16), 'tensor')]
    dot_general x80 -> x0, matrix products: 74.7 us -> none  [the longest x68 65.8 us: matmul(): return jnp.dot(left, right, preferred_element_type=jnp.float32)]
    all_to_all x8 -> x0, waiting for transfers between devices: 71.2 us -> none  [the longest x2 29.1 us: body(): lax.all_to_all(to_owners(grad_pairs_out, source), 'expert', split_axis=0,...]
    unnamed x2 -> x0, blocking collectives: 43.4 us -> none
  transfers between devices with their start and end apart: 21 -> 0, of which waited for: 18 -> 0; matrix products, arithmetic and copies ran while one was open for 8% -> 0% of each run, Pallas kernels for 0% -> 0%
where the time goes in v1:
time: 291 us; the launch traced here: 290 us
  Pallas kernels  269 us (92%)
  local copies, waits for them, and re-layouts  21 us (7%)
    pallas_call x1, Pallas kernels, fused_body(): pl.pallas_call(functools.partial(layer_kernel, s, names), out_shape=(shap...  269 us
    unnamed x20, local copies, waits for them, and re-layouts  12.8 us

profile of v1, /device:TPU:0, one launch (start us, length us, event | category | flops | bytes accessed | tf_op | source)
XLA Modules:
  0.0 290.3 jit_solution(20295002595357394)
XLA Ops:
  0.6 0.8 copy.35
  1.4 0.8 copy.36
  2.2 0.8 copy.37
  3.0 0.7 concatenate.3.refs_9_
  3.7 1.5 copy.34
  5.2 1.5 copy.33
  6.7 268.6 %shard_map.289 = (bf16[256,768]{1,0:T(8,128)(2,1)}, f32[256,768]{1,0:T(8,128)}, f32[3,96,192]{2,1,0:T(8,128)}, f32[96,192]{1,0:T(8,128)}, f32[96,128]{1,0:T(8,12...) custom-call(bf16[256,768]{1,0:T(8,128)(2,1)} %bitcast.42, ...), custom_call_target="tpu_custom_call" | custom-call | tf_op jit(solution)/shard_map/pallas_call | solution.py:1348
  275.3 0.0 copy-start.4
  275.3 0.0 copy-start.3
  275.3 1.3 slice_bitcast_fusion.6
  276.6 0.9 slice.32
  277.5 0.7 copy.39
  278.1 1.6 copy.38
  279.8 1.7 slice_bitcast_fusion.3
  281.5 0.0 copy-start.2
  281.5 2.1 slice_bitcast_fusion
  283.5 0.0 copy-done.4
  283.5 0.7 copy.45
  284.3 0.0 copy-done.3
  284.3 0.9 copy.46
  285.2 0.0 copy-done.2
  285.2 0.0 copy-start.1
  285.2 1.1 copy.47
  286.3 0.8 copy-done.1
  287.1 0.0 copy-start
  287.1 1.1 copy.48
  288.3 0.8 copy-done
  289.1 1.1 copy.49
  (2 shorter events, 0.0 us)
Async XLA Ops:
  275.3 8.2 %copy-start.4 = (bf16[256,768]{1,0:T(8,128)(2,1)S(1)}, bf16[256,768]{1,0:T(8,128)(2,1)}, u32[]{:S(2)}) copy-start(bf16[256,768]{1,0:T(8,128)(2,1)} %get-tuple-element.25) | copy-start | bytes 1179652
  275.3 9.0 %copy-start.3 = (f32[256,768]{1,0:T(8,128)S(1)}, f32[256,768]{1,0:T(8,128)}, u32[]{:S(2)}) copy-start(f32[256,768]{1,0:T(8,128)} %get-tuple-element.26) | copy-start | bytes 2359300
  281.5 3.7 %copy-start.2 = (f32[768,512]{1,0:T(8,128)S(1)}, f32[768,512]{1,0:T(8,128)}, u32[]{:S(2)}) copy-start(f32[768,512]{1,0:T(8,128)} %get-tuple-element.32) | copy-start | bytes 4718596
  285.2 2.0 copy-start.1
  287.1 2.0 copy-start

commit v2 on v0

--- a/solution.py
+++ b/solution.py
@@ -1,8 +1,12 @@
+import functools
 import math
+import types
 
 import jax
 import jax.numpy as jnp
 from jax import lax
+from jax.experimental import pallas as pl
+from jax.experimental.pallas import tpu as pltpu
 from jax.sharding import PartitionSpec as P
 
 HEAD = 64
@@ -110,7 +114,7 @@
     return (weights_exp * (grad_exp - jnp.transpose(delta_rows)[:, :, None])).astype(jnp.bfloat16)
 
 
-def body(
+def plain_body(
     tokens,
     out_grad,
     routes,
@@ -459,6 +463,1121 @@
     )
 
 
+MESH = pl.DeviceIdType.MESH
+BF = jnp.bfloat16
+F32 = jnp.float32
+EXACT = lax.Precision.HIGHEST
+VMEM_LIMIT = 63 * 2**20
+
+
+def product(left, right, dims, precision=None):
+    return lax.dot_general(
+        left, right, (dims, ((), ())), preferred_element_type=F32, precision=precision
+    )
+
+
+def dot(left, right, precision=None):
+    return product(left, right, ((1,), (0,)), precision)
+
+
+def dot_nt(left, right, precision=None):
+    return product(left, right, ((1,), (1,)), precision)
+
+
+def dot_tn(left, right, precision=None):
+    return product(left, right, ((0,), (0,)), precision)
+
+
+def iota(shape, dim):
+    return lax.broadcasted_iota(jnp.int32, shape, dim)
+
+
+class Net:
+    def __init__(self, expert_size, send_sems, recv_sems):
+        self.e = lax.axis_index("expert")
+        self.t = lax.axis_index("tensor")
+        self.n = expert_size
+        self.nz = expert_size // 2
+        self.z = self.e // 2
+        self.x = self.e % 2
+        self.y = self.t // 2
+        self.core = self.t % 2
+        self.send_sems = send_sems
+        self.recv_sems = recv_sems
+        self.sends = 0
+        self.recvs = 0
+        self.open = []
+
+    def recv_slots(self, count):
+        first = self.recvs
+        self.recvs += count
+        return first
+
+    def ids(self, to):
+        return {"expert": to[0], "tensor": to[1]}
+
+    def push(self, src, dst, to, slot, when=None):
+        copy = pltpu.make_async_remote_copy(
+            src_ref=src,
+            dst_ref=dst,
+            send_sem=self.send_sems.at[self.sends],
+            recv_sem=self.recv_sems.at[slot],
+            device_id=self.ids(to),
+            device_id_type=MESH,
+        )
+        self.sends += 1
+        if when is None:
+            copy.start()
+        else:
+            pl.when(when)(copy.start)
+        self.open.append((copy, when))
+
+    def landed(self, dst, slot, when=None):
+        copy = pltpu.make_async_remote_copy(
+            src_ref=dst,
+            dst_ref=dst,
+            send_sem=self.send_sems.at[0],
+            recv_sem=self.recv_sems.at[slot],
+            device_id=self.ids(self.other_core()),
+            device_id_type=MESH,
+        )
+        if when is None:
+            copy.wait_recv()
+        else:
+            pl.when(when)(copy.wait_recv)
+
+    def drain(self, first=0, last=None):
+        last = len(self.open) if last is None else last
+        for copy, when in self.open[first:last]:
+            if when is None:
+                copy.wait_send()
+            else:
+                pl.when(when)(copy.wait_send)
+        self.open[first:last] = []
+
+    def other_core(self):
+        return (self.e, self.t + 1 - 2 * self.core)
+
+    def across_y(self):
+        return (self.e, (self.t + 2) % 4)
+
+    def across_x(self):
+        return (self.e + 1 - 2 * self.x, self.t)
+
+    def peer(self, step):
+        return (self.e + step) % self.n
+
+    def greet(self):
+        barrier = pltpu.get_barrier_semaphore()
+        partners = [(self.peer(d), self.t) for d in range(1, self.n)]
+        partners += [self.other_core(), self.across_y()]
+        for to in partners:
+            pl.semaphore_signal(barrier, inc=1, device_id=self.ids(to), device_id_type=MESH)
+        return lambda: pl.semaphore_wait(barrier, len(partners))
+
+
+class Gather:
+    def __init__(self, net, block, chunks=1, on_land=None):
+        self.net, self.block, self.chunks, self.on_land = net, block, chunks, on_land
+        self.slot = net.recv_slots(net.n * chunks)
+
+    def start(self):
+        net = self.net
+        for k in range(self.chunks):
+            own, slot = self.block(net.e, k), self.slot + net.e * self.chunks + k
+            for way in (1, -1):
+                there = net.z + way
+                fits_in = (there >= 0) & (there < net.nz)
+                net.push(own, own, (there % net.nz * 2 + net.x, net.t), slot, fits_in)
+            net.push(own, own, net.across_x(), slot)
+
+    def step(self, distance):
+        net = self.net
+        for k in range(self.chunks):
+            for way in (1, -1):
+                source, there = net.z - way * distance, net.z + way
+                real = (source >= 0) & (source < net.nz)
+                onward = real & (there >= 0) & (there < net.nz)
+                b = source % net.nz * 2 + net.x
+                part, slot = self.block(b, k), self.slot + b * self.chunks + k
+                net.landed(part, slot, real)
+                net.push(part, part, (there % net.nz * 2 + net.x, net.t), slot, onward)
+                net.push(part, part, net.across_x(), slot, real)
+                if self.on_land is not None:
+                    self.on_land(b, real)
+
+    def finish(self):
+        net = self.net
+        for d in range(net.nz):
+            b = (net.z + d) % net.nz * 2 + 1 - net.x
+            for k in range(self.chunks):
+                net.landed(self.block(b, k), self.slot + b * self.chunks + k)
+            if self.on_land is not None:
+                self.on_land(b, None)
+
+
+class Scatter:
+    def __init__(self, net, block, from_x, from_z):
+        self.net, self.block = net, block
+        self.from_x, self.from_z = from_x, from_z
+        self.slot_x = net.recv_slots(net.nz)
+        self.slot_z = net.recv_slots(net.nz)
+
+    def start(self):
+        net = self.net
+        for d in range(1, net.nz + 1):
+            zz = (net.z + d) % net.nz
+            net.push(
+                self.block(zz * 2 + 1 - net.x), self.from_x.at[zz], net.across_x(), self.slot_x + zz
+            )
+
+    def forward(self):
+        net = self.net
+        for d in range(1, net.nz):
+            zz = (net.z + d) % net.nz
+            net.landed(self.from_x.at[zz], self.slot_x + zz)
+            pair = self.block(zz * 2 + net.x)[...].astype(F32) + self.from_x[zz].astype(F32)
+            self.from_x[zz] = pair.astype(BF)
+            net.push(
+                self.from_x.at[zz],
+                self.from_z.at[net.z],
+                (zz * 2 + net.x, net.t),
+                self.slot_z + net.z,
+            )
+
+    def finish(self):
+        net = self.net
+        net.landed(self.from_x.at[net.z], self.slot_x + net.z)
+        total = self.block(net.e)[...].astype(F32) + self.from_x[net.z].astype(F32)
+        for d in range(1, net.nz):
+            zz = (net.z + d) % net.nz
+            net.landed(self.from_z.at[zz], self.slot_z + zz)
+            total = total + self.from_z[zz].astype(F32)
+        return total
+
+
+class Exchange:
+    def __init__(self, net, outgoing, incoming):
+        self.net, self.outgoing, self.incoming = net, outgoing, incoming
+        self.slot = net.recv_slots(net.n)
+
+    def start(self):
+        net = self.net
+        for d in range(1, net.n):
+            to = net.peer(d)
+            net.push(self.outgoing(to), self.incoming(net.e), (to, net.t), self.slot + net.e)
+
+    def arrive(self, d):
+        source = self.net.peer(d)
+        self.net.landed(self.incoming(source), self.slot + source)
+        return source
+
+    def finish(self):
+        for d in range(1, self.net.n):
+            self.arrive(d)
+
+
+class Dispatch:
+    def __init__(self, net, outgoing, incoming):
+        self.net, self.outgoing, self.incoming = net, outgoing, incoming
+        self.send = Exchange(
+            net, lambda b: outgoing.at[b], lambda b: incoming.at[b, net.core, net.y]
+        )
+        self.slot_y = net.recv_slots(net.n)
+        self.slot_core = net.recv_slots(1)
+
+    def start(self):
+        net = self.net
+        self.send.start()
+        self.incoming[net.e, net.core, net.y] = self.outgoing[net.e]
+
+    def relay_y(self):
+        net = self.net
+        for d in range(net.n):
+            b = net.e if d == 0 else self.send.arrive(d)
+            part = self.incoming.at[b, net.core, net.y]
+            net.push(part, part, net.across_y(), self.slot_y + b)
+
+    def relay_core(self):
+        net = self.net
+        for d in range(net.n):
+            b = net.peer(d)
+            net.landed(self.incoming.at[b, net.core, 1 - net.y], self.slot_y + b)
+        part = self.incoming.at[:, net.core]
+        net.push(part, part, net.other_core(), self.slot_core)
+
+    def finish(self):
+        self.net.landed(self.incoming.at[:, 1 - self.net.core], self.slot_core)
+
+
+class Swap:
+    def __init__(self, net, out_buf, in_buf, partner):
+        self.net, self.out_buf, self.in_buf, self.partner = net, out_buf, in_buf, partner
+        self.slot = net.recv_slots(1)
+
+    def start(self, value):
+        self.out_buf[...] = value.astype(self.out_buf.dtype)
+        self.send()
+
+    def send(self):
+        self.net.push(self.out_buf, self.in_buf, self.partner, self.slot)
+
+    def other(self):
+        self.net.landed(self.in_buf, self.slot)
+        return self.in_buf[...].astype(F32)
+
+    def both(self):
+        return self.out_buf[...].astype(F32) + self.other()
+
+
+class Share:
+    def __init__(self, net, halves):
+        self.net, self.halves = net, halves
+        self.slot = net.recv_slots(1)
+
+    def start(self, value):
+        net = self.net
+        self.halves[net.core] = value.astype(self.halves.dtype)
+        part = self.halves.at[net.core]
+        net.push(part, part, net.other_core(), self.slot)
+
+    def finish(self):
+        net = self.net
+        net.landed(self.halves.at[1 - net.core], self.slot)
+        return jnp.concatenate([self.halves[0], self.halves[1]], axis=1)
+
+
+def silu_both(value):
+    gate = jax.nn.sigmoid(value)
+    return value * gate, gate * (1.0 + value * (1.0 - gate))
+
+
+def norm_scale(value):
+    return lax.rsqrt(jnp.mean(value * value, axis=1, keepdims=True) + EPSILON)
+
+
+def norm_back(grad_normed, source, scale, gain):
+    weighted = grad_normed * gain
+    inner = jnp.mean(weighted * source, axis=1, keepdims=True)
+    return scale * weighted - scale * scale * scale * source * inner
+
+
+PLACES = ["tok", "cot", "routes", "lengths", "parents", "gain_a", "gain_b", "wq", "wk", "wv"]
+PLACES += ["wo", "router", "sg", "su", "sd", "eg", "eu", "ed"]
+RESULTS = ["out", "gtok", "dga", "dgb", "dwq", "dwk", "dwv", "dwo", "drouter"]
+RESULTS += ["dsg", "dsu", "dsd", "deg", "deu", "ded"]
+
+
+def scratch_shapes(s):
+    n, local, half = s.n, s.local, s.half
+    depth, hidden, shared, cap = s.depth, s.hidden, s.shared, s.cap
+    micro, nz = s.micro, s.n // 2
+    model, wide, stack, tree = 2 * half, 2 * s.width, s.heads * local, n * local
+    part = cap // 4
+    vm = pltpu.VMEM
+    return dict(
+        w_kv=vm((n, depth, wide), BF),
+        w_qo=vm((n, depth, wide), BF),
+        w_sh=vm((3, n, depth, shared), BF),
+        ext_in=vm((n, 16, 128), BF),
+        tok_all=vm((n, 2, 2, micro * local // 4, model), BF),
+        cos_all=vm((n, micro * local, 128), F32),
+        sin_all=vm((n, micro * local, 128), F32),
+        kv=vm((micro, n, local, wide), BF),
+        q_rows=vm((micro, stack, wide), BF),
+        expo=vm((micro, stack, tree), F32),
+        total=vm((micro, stack, 1), F32),
+        mixed=vm((micro, local, wide), F32),
+        mixed_low=vm((micro * local, wide), BF),
+        choice=vm((micro, local, n * cap), BF),
+        choice_wide=vm((micro, local, n * 128), BF),
+        res=vm((micro, local, model), F32),
+        n_one=vm((micro * local, model), BF),
+        n_two=vm((micro * local, model), BF),
+        c_out=vm((micro, n, part, model), BF),
+        c_in=vm((micro, n, 2, 2, part, model), BF),
+        x_out=vm((micro, n, part, model), BF),
+        x_in=vm((micro, n, 2, 2, part, model), BF),
+        h_out=vm((micro, n, 16, 128), BF),
+        h_in=vm((micro, n, 16, 128), BF),
+        gate_col=vm((micro, n * cap, 1), F32),
+        e_h=vm((micro, n * cap, hidden), BF),
+        e_dg=vm((micro, n * cap, hidden), BF),
+        e_du=vm((micro, n * cap, hidden), BF),
+        y_core=vm((micro, n, cap, half), BF),
+        g_core=vm((micro, n, cap, half), BF),
+        y_in=vm((micro, n, cap, half), BF),
+        g_in=vm((micro, n, cap, half), BF),
+        d_out=vm((micro, n, 8, 128), F32),
+        d_in=vm((micro, n, 8, 128), F32),
+        d_tensor=vm((micro, 4, 8, 128), F32),
+        core_a=vm((micro, 2, local, half), F32),
+        core_b=vm((4, micro * local, half), BF),
+        core_c=vm((micro, 2, local, half), F32),
+        s_grads=vm((3, micro * local, shared), BF),
+        s_own=vm((2, micro * local, half), F32),
+        y_swap=vm((4, micro, 2, local, half), BF),
+        share_a=vm((micro, 2, local, half), F32),
+        share_b=vm((micro, 2, local, half), F32),
+        share_c=vm((micro, 2, local, half), F32),
+        share_out=vm((micro, 2, local, half), BF),
+        kv_part=vm((micro, n, local, wide), BF),
+        kv_fx=vm((micro, nz, local, wide), BF),
+        kv_fz=vm((micro, nz, local, wide), BF),
+        sh_part=vm((3, n, depth, shared), BF),
+        sh_fx=vm((3, nz, depth, shared), BF),
+        sh_fz=vm((3, nz, depth, shared), BF),
+        w_part=vm((2, n, depth, wide), BF),
+        w_fx=vm((2, nz, depth, wide), BF),
+        w_fz=vm((2, nz, depth, wide), BF),
+        gains_out=vm((n, 16, 128), F32),
+        gains_in=vm((n, 16, 128), F32),
+        stage=vm((2, half, hidden), F32),
+        stage_d=vm((hidden, half), F32),
+        save_sems=pltpu.SemaphoreType.DMA((6,)),
+        send_sems=pltpu.SemaphoreType.DMA((SENDS,)),
+        recv_sems=pltpu.SemaphoreType.DMA((RECVS,)),
+    )
+
+
+SENDS = 400
+RECVS = 400
+
+
+def layer_kernel(s, names, *refs):
+    r = types.SimpleNamespace(**dict(zip(names, refs)))
+    n, local, width, half = s.n, s.local, s.width, s.half
+    depth, hidden, shared, cap = s.depth, s.hidden, s.shared, s.cap
+    micro, heads = s.micro, s.heads
+    rows, model, tree, wide, stack = micro * local, 2 * half, n * local, 2 * width, heads * local
+    part = cap // 4
+    net = Net(n, r.send_sems, r.recv_sems)
+    me, core, y = net.e, net.core, net.y
+    ready = net.greet()
+    micros = range(micro)
+    my_half = pl.ds(pl.multiple_of(core * half, 128), half)
+    other_half = pl.ds(pl.multiple_of((1 - core) * half, 128), half)
+
+    def rows_of(m):
+        return slice(m * local, (m + 1) * local)
+
+    left = (iota((width, wide), 1) == iota((width, wide), 0)).astype(BF)
+    right = (iota((width, wide), 1) == iota((width, wide), 0) + width).astype(BF)
+    r.w_kv[me] = (dot(r.wk[...], left) + dot(r.wv[...], right)).astype(BF)
+    r.tok_all[me] = r.tok[...].reshape(2, 2, rows // 4, model)
+    r.w_qo[me] = (dot(r.wq[...], left) + dot_tn(r.wo[...], right)).astype(BF)
+    ext = [r.gain_a[...].astype(F32), r.gain_b[...].astype(F32), jnp.zeros((6, depth), F32)]
+    ext = jnp.concatenate(ext + [r.router[...].astype(F32)], axis=0).astype(BF)
+    pad = (iota((depth, 128), 1) == iota((depth, 128), 0)).astype(BF)
+    r.ext_in[me] = dot(ext, pad).astype(BF)
+    for i, name in enumerate(("sg", "su", "sd")):
+        r.w_sh[i, me] = getattr(r, name)[...]
+
+    slot_ty, slot_tc = net.recv_slots(n), net.recv_slots(n)
+
+    def token_on(b, when):
+        quarter = r.tok_all.at[b, core, y]
+        net.push(quarter, quarter, net.across_y(), slot_ty + b, when)
+
+    get_kv = Gather(net, lambda b, k: r.w_kv.at[b])
+    get_qo = Gather(net, lambda b, k: r.w_qo.at[b])
+    get_tok = Gather(net, lambda b, k: r.tok_all.at[b, core, y], on_land=token_on)
+    get_sh = [Gather(net, lambda b, k, i=i: r.w_sh.at[i, b]) for i in range(3)]
+    get_ext = Exchange(net, lambda b: r.ext_in.at[me], lambda b: r.ext_in.at[b])
+    ready()
+    get_ext.start()
+    get_tok.start()
+    get_kv.start()
+    get_qo.start()
+
+    eye = (iota((128, 128), 0) == iota((128, 128), 1)).astype(BF)
+    routes = dot_nt(eye, r.routes[...].astype(BF))
+    lane = iota((local, 16), 1) - 8
+    earlier = (iota((local, local), 1) < iota((local, local), 0)).astype(BF)
+
+    def spread(span):
+        of_lane = iota((16, n * span), 1) // span
+        return (iota((16, n * span), 0) - 8 == of_lane).astype(BF)
+
+    hot_one, hot_two, quarter = [], [], []
+    send_c = [Dispatch(net, r.c_out.at[m], r.c_in.at[m]) for m in micros]
+    send_h = [
+        Exchange(net, lambda b, m=m: r.h_out.at[m, b], lambda b, m=m: r.h_in.at[m, b])
+        for m in micros
+    ]
+    for m in micros:
+        one = lane == routes[:, 2 * m : 2 * m + 1].astype(jnp.int32)
+        two = lane == routes[:, 2 * m + 1 : 2 * m + 2].astype(jnp.int32)
+        hot_one.append(one)
+        hot_two.append(two)
+        hits = (one | two).astype(F32)
+        rank = jnp.where(hits > 0.5, dot(earlier, hits.astype(BF)), -1.0).astype(BF)
+
+        def taken(span, first=0):
+            wanted = iota((local, n * span), 1) % span + first
+            return (dot(rank, spread(span)) == wanted.astype(F32)).astype(BF)
+
+        r.choice[m] = taken(cap)
+        r.choice_wide[m] = taken(128)
+        quarter.append(taken(part, (core * 2 + y) * part))
+        hit_rows = dot_tn(hits.astype(BF), r.choice_wide[m]).astype(BF)
+        for b in range(n):
+            r.h_out[m, b] = hit_rows[:, b * 128 : (b + 1) * 128]
+        r.h_in[m, me] = r.h_out[m, me]
+        picked = dot_tn(quarter[m], r.cot[rows_of(m)]).astype(BF)
+        r.c_out[m] = picked.reshape(n, part, model)
+
+    def segments(m):
+        starts, ends, paths, shifts, begin = [], [], [], [], 0
+        for seg in range(s.segs):
+            size = r.lengths[m, seg]
+            starts.append(begin)
+            ends.append(begin + size)
+            begin = begin + size
+            if seg == 0:
+                paths.append(jnp.int32(1))
+                shifts.append(jnp.int32(0))
+            else:
+                parent = r.parents[m, seg]
+                path, shift = jnp.int32(0), jnp.int32(0)
+                for other in range(seg):
+                    is_parent = parent == other
+                    path = jnp.where(is_parent, paths[other], path)
+                    shift = jnp.where(
+                        is_parent, shifts[other] + ends[other] - starts[other], shift
+                    )
+                paths.append(path + (1 << seg))
+                shifts.append(shift)
+        return starts, ends, paths, shifts
+
+    tables = [segments(m) for m in micros]
+
+    def row_values(m, ids):
+        starts, ends, paths, shifts = tables[m]
+        path, place, own = jnp.zeros_like(ids), jnp.zeros_like(ids), jnp.zeros_like(ids)
+        for seg in range(s.segs):
+            inside = (ids >= starts[seg]) & (ids < ends[seg])
+            path = jnp.where(inside, paths[seg], path)
+            place = jnp.where(inside, ids - starts[seg] + shifts[seg], place)
+            own = jnp.where(inside, 1 << seg, own)
+        return path, place, own
+
+    turn = (iota((1, 128), 1) % (HEAD // 2)).astype(F32)
+    frequency = jnp.exp(turn * (-math.log(ROPE_BASE) / (HEAD // 2)))
+
+    def angle_step(b, carry):
+        ids = b * local + iota((local, 1), 0)
+        place = jnp.concatenate([row_values(m, ids)[1] for m in micros], axis=0)
+        angle = place.astype(F32) * frequency
+        r.cos_all[b] = jnp.cos(angle)
+        r.sin_all[b] = jnp.sin(angle)
+        return carry
+
+    lax.fori_loop(0, n, angle_step, 0)
+    is_left = iota((1, wide), 1) < width
+    swap_r, swap_c = iota((wide, wide), 0), iota((wide, wide), 1)
+    lower = swap_c % HEAD < HEAD // 2
+    swap = jnp.where(lower & (swap_r == swap_c + HEAD // 2), -1.0, 0.0)
+    swap = jnp.where(~lower & (swap_r == swap_c - HEAD // 2), 1.0, swap)
+    swap = jnp.where(is_left, swap, 0.0)
+    swap_low = swap.astype(BF)
+
+    def turns(b):
+        cosine = jnp.concatenate([r.cos_all[b]] * (wide // 128), axis=1)
+        sine = jnp.concatenate([r.sin_all[b]] * (wide // 128), axis=1)
+        return jnp.where(is_left, cosine, 1.0), sine
+
+    for distance in range(1, net.nz):
+        get_tok.step(distance)
+        get_kv.step(distance)
+        get_qo.step(distance)
+    get_tok.finish()
+    get_ext.finish()
+    for d in range(1, n):
+        b = net.peer(d)
+        net.landed(r.tok_all.at[b, core, 1 - y], slot_ty + b)
+        both = r.tok_all.at[b, core]
+        net.push(both, both, net.other_core(), slot_tc + b)
+
+    def lay(b):
+        place = iota((128, model), 0)
+        return (place < depth) & (place + b * depth == iota((128, model), 1))
+
+    ext_all = jnp.zeros((16, model), F32)
+    for b in range(n):
+        ext_all = ext_all + dot(r.ext_in[b], lay(b).astype(BF))
+    gain_one, gain_two = ext_all[0:1], ext_all[1:2]
+    ext_low = ext_all.astype(BF)
+    get_kv.finish()
+    w_kv = r.w_kv[...].reshape(model, wide)
+    w_kv_swapped = dot(w_kv, swap_low).astype(BF)
+
+    def normed(block):
+        value = block.astype(F32)
+        return (value * norm_scale(value) * gain_one).astype(BF)
+
+    def key_value(b):
+        block = normed(r.tok_all[b].reshape(rows, model))
+        cosine, sine = turns(b)
+        both = (dot(block, w_kv) * cosine + dot(block, w_kv_swapped) * sine).astype(BF)
+        for m in micros:
+            r.kv[m, b] = both[rows_of(m)]
+
+    key_value(me)
+
+    def key_value_step(d, carry):
+        b = net.peer(d)
+        net.landed(r.tok_all.at[b, 1 - core], slot_tc + b)
+        key_value(b)
+        return carry
+
+    lax.fori_loop(1, n, key_value_step, 0)
+    get_qo.finish()
+    r.n_one[...] = normed(r.tok[...])
+    w_qo = r.w_qo[...].reshape(model, wide)
+    cosine, sine = turns(me)
+    cosine = jnp.where(is_left, cosine, 0.0)
+    queries = dot(r.n_one[...], w_qo) * cosine
+    queries = queries + dot(r.n_one[...], dot(w_qo, swap_low).astype(BF)) * sine
+    queries = queries.astype(BF)
+    for m in micros:
+        send_c[m].start()
+        send_h[m].start()
+    get_sh[0].start()
+
+    head_of = iota((1, wide), 1) // HEAD
+    q_masks = [head_of == h for h in range(heads)]
+    v_masks = [head_of == heads + h for h in range(heads)]
+
+    def by_head(block, masks):
+        return jnp.concatenate(
+            [jnp.where(mask, block, jnp.zeros_like(block)) for mask in masks], axis=0
+        )
+
+    def join_heads(value, masks):
+        total = jnp.zeros((local, wide), F32)
+        for h, mask in enumerate(masks):
+            total = total + jnp.where(mask, value[h * local : (h + 1) * local], 0.0)
+        return total
+
+    def o_half(h):
+        return r.w_qo[pl.ds(h * (n // 2), n // 2)].reshape(half, wide)
+
+    core_a = [Swap(net, r.core_a.at[m, 0], r.core_a.at[m, 1], net.other_core()) for m in micros]
+    core_c = [Swap(net, r.core_c.at[m, 0], r.core_c.at[m, 1], net.other_core()) for m in micros]
+    core_b = [
+        Swap(net, r.core_b.at[2 * i], r.core_b.at[2 * i + 1], net.other_core()) for i in range(2)
+    ]
+    y_swap = [
+        [Swap(net, r.y_swap.at[i, m, 0], r.y_swap.at[i, m, 1], net.across_y()) for m in micros]
+        for i in range(4)
+    ]
+    share_a = [Share(net, r.share_a.at[m]) for m in micros]
+    share_b = [Share(net, r.share_b.at[m]) for m in micros]
+    share_c = [Share(net, r.share_c.at[m]) for m in micros]
+    share_out = [Share(net, r.share_out.at[m]) for m in micros]
+
+    score_scale = HEAD**-0.5
+    for m in micros:
+        r.q_rows[m] = by_head(queries[rows_of(m)], q_masks)
+        kv_rows = r.kv[m].reshape(tree, wide)
+        ids = me * local + iota((stack, 1), 0) % local
+        path, unused, unused_two = row_values(m, ids)
+        key_ids = iota((1, tree), 1)
+        unused, unused_two, key_seg = row_values(m, key_ids)
+        seen = ((path & key_seg) != 0) & (key_ids <= ids)
+        scores = dot_nt(r.q_rows[m], kv_rows) * score_scale
+        expo = jnp.where(seen, jnp.exp(scores), 0.0)
+        r.expo[m] = expo
+        total = jnp.sum(expo, axis=1, keepdims=True)
+        r.total[m] = total
+        mixed = join_heads(dot(expo.astype(BF), kv_rows) / total, v_masks)
+        r.mixed[m] = mixed
+        r.mixed_low[rows_of(m)] = mixed.astype(BF)
+        core_a[m].start(dot_nt(r.mixed_low[rows_of(m)], o_half(1 - core)))
+    for m in micros:
+        mine = dot_nt(r.mixed_low[rows_of(m)], o_half(core))
+        y_swap[0][m].start(mine + core_a[m].other())
+    get_sh[0].step(1)
+    for m in micros:
+        send_c[m].relay_y()
+    for m in micros:
+        share_a[m].start(y_swap[0][m].both())
+
+    send_x = [Dispatch(net, r.x_out.at[m], r.x_in.at[m]) for m in micros]
+    scale_two = []
+    for m in micros:
+        res = r.tok[rows_of(m)].astype(F32) + share_a[m].finish()
+        r.res[m] = res
+        scale_two.append(norm_scale(res))
+        normed_two = (res * scale_two[m] * gain_two).astype(BF)
+        r.n_two[rows_of(m)] = normed_two
+        r.x_out[m] = dot_tn(quarter[m], normed_two).astype(BF).reshape(n, part, model)
+        send_x[m].start()
+
+    gates = []
+    for m in micros:
+        logits = dot_nt(r.n_two[rows_of(m)], ext_low)
+        z_one = jnp.sum(jnp.where(hot_one[m], logits, 0.0), axis=1, keepdims=True)
+        z_two = jnp.sum(jnp.where(hot_two[m], logits, 0.0), axis=1, keepdims=True)
+        z_top = jnp.maximum(z_one, z_two)
+        e_one, e_two = jnp.exp(z_one - z_top), jnp.exp(z_two - z_top)
+        chosen = jnp.where(hot_one[m], e_one, jnp.where(hot_two[m], e_two, 0.0))
+        gates.append(chosen / (e_one + e_two))
+    for m in micros:
+        send_c[m].relay_core()
+    get_sh[0].step(2)
+    get_sh[0].step(3)
+    for m in micros:
+        send_x[m].relay_y()
+    get_sh[1].start()
+    get_sh[2].start()
+    for m in micros:
+        send_x[m].relay_core()
+    for m in micros:
+        send_h[m].finish()
+        send_c[m].finish()
+
+    slot_gc = net.recv_slots(micro)
+    slot_yc = net.recv_slots(micro)
+    send_g = [
+        Exchange(net, lambda b, m=m: r.g_core.at[m, b], lambda b, m=m: r.g_in.at[m, b])
+        for m in micros
+    ]
+    send_y = [
+        Exchange(net, lambda b, m=m: r.y_core.at[m, b], lambda b, m=m: r.y_in.at[m, b])
+        for m in micros
+    ]
+    send_d = [
+        Exchange(net, lambda b, m=m: r.d_out.at[m, b], lambda b, m=m: r.d_in.at[m, b])
+        for m in micros
+    ]
+    slot_eye = eye[:cap]
+    slot_line = iota((cap, 128), 0) == iota((cap, 128), 1)
+    own_lane = iota((n * cap, 16), 1) - 8 == me
+    group = 4
+    halves = [slice(0, half), slice(half, model)]
+
+    def expert(m):
+        x_rows = r.x_in[m].reshape(n * cap, model)
+        z_all = dot_nt(x_rows, ext_low)
+        hit = jnp.concatenate([dot_nt(slot_eye, r.h_in[m, b]) for b in range(n)], axis=0)
+        z_own = jnp.sum(jnp.where(own_lane, z_all, 0.0), axis=1, keepdims=True)
+        z_other = jnp.sum(jnp.where(own_lane, 0.0, z_all * hit), axis=1, keepdims=True)
+        z_top = jnp.maximum(z_own, z_other)
+        e_own, e_other = jnp.exp(z_own - z_top), jnp.exp(z_other - z_top)
+        r.gate_col[m] = e_own / (e_own + e_other)
+        count = group * cap
+
+        def step(i, carry):
+            span = pl.ds(i * group, group)
+            flat = pl.ds(pl.multiple_of(i * count, count), count)
+            x = r.x_in[m, span].reshape(count, model)
+            c = r.c_in[m, span].reshape(count, model)
+            gate = r.gate_col[m, flat]
+            gate_pre = dot(x, r.eg[...])
+            up_pre = dot(x, r.eu[...])
+            act, slope = silu_both(gate_pre)
+            hid = (act * up_pre).astype(BF)
+            grad_y = (gate * c.astype(F32)).astype(BF)
+            grad_hid = dot_nt(grad_y, r.ed[...])
+            grad_g = (grad_hid * up_pre * slope).astype(BF)
+            grad_u = (grad_hid * act).astype(BF)
+            r.e_h[m, flat] = hid
+            r.e_dg[m, flat] = grad_g
+            r.e_du[m, flat] = grad_u
+            dots = jnp.zeros((count, 1), F32)
+            for cut in halves:
+                out = dot(hid, r.ed[:, cut])
+                r.tok_all[span, 0, m, :, cut] = out.astype(BF).reshape(group, cap, half)
+                dots = dots + jnp.sum(out * c[:, cut].astype(F32), axis=1, keepdims=True)
+                back = dot_nt(grad_g, r.eg[cut]) + dot_nt(grad_u, r.eu[cut])
+                r.tok_all[span, 1, m, :, cut] = back.astype(BF).reshape(group, cap, half)
+            r.c_in[m, span] = grad_y.reshape(group, 2, 2, part, model)
+            for b in range(group):
+                line = jnp.where(slot_line, dots[b * cap : (b + 1) * cap], 0.0)
+                line = jnp.sum(line, axis=0, keepdims=True)
+                r.d_out[m, i * group + b] = jnp.broadcast_to(line, (8, 128))
+            return carry
+
+        lax.fori_loop(0, n // group, step, 0)
+        net.push(r.tok_all.at[:, 1, m, :, other_half], r.g_core.at[m], net.other_core(), slot_gc + m)
+        net.push(r.tok_all.at[:, 0, m, :, other_half], r.y_core.at[m], net.other_core(), slot_yc + m)
+
+    def return_g(m):
+        send_d[m].start()
+        r.d_in[m, me] = r.d_out[m, me]
+        net.landed(r.g_core.at[m], slot_gc + m)
+        r.g_core[m] = (r.tok_all[:, 1, m, :, my_half].astype(F32) + r.g_core[m].astype(F32)).astype(BF)
+        send_g[m].start()
+        r.g_in[m, me] = r.g_core[m, me]
+
+    def return_y(m):
+        net.landed(r.y_core.at[m], slot_yc + m)
+        r.y_core[m] = (r.tok_all[:, 0, m, :, my_half].astype(F32) + r.y_core[m].astype(F32)).astype(BF)
+        send_y[m].start()
+        r.y_in[m, me] = r.y_core[m, me]
+
+    net.drain()
+    for m in micros:
+        send_x[m].finish()
+        expert(m)
+    for m in micros:
+        return_g(m)
+
+    for distance in range(1, net.nz):
+        get_sh[1].step(distance)
+        get_sh[2].step(distance)
+    for g in get_sh:
+        g.finish()
+
+    def wide_half(i, h):
+        return r.w_sh[i, pl.ds(h * (n // 2), n // 2)].reshape(half, shared)
+
+    def shared_step(m, carry):
+        here = pl.ds(pl.multiple_of(m * local, local), local)
+        normed_two = r.n_two[here]
+        shared_g = dot(normed_two, r.w_sh[0].reshape(model, shared))
+        shared_u = dot(normed_two, r.w_sh[1].reshape(model, shared))
+        act, slope = silu_both(shared_g)
+        shared_h = (act * shared_u).astype(BF)
+        grad_h = dot(r.cot[here], r.w_sh[2].reshape(model, shared))
+        grad_g = (grad_h * shared_u * slope).astype(BF)
+        grad_u = (grad_h * act).astype(BF)
+        r.s_grads[0, here] = grad_g
+        r.s_grads[1, here] = grad_u
+        r.s_grads[2, here] = shared_h
+        other, own = 1 - core, core
+        back = dot_nt(grad_g, wide_half(0, other)) + dot_nt(grad_u, wide_half(1, other))
+        r.core_b[0, here] = back.astype(BF)
+        r.core_b[2, here] = dot_nt(shared_h, wide_half(2, other)).astype(BF)
+        back = dot_nt(grad_g, wide_half(0, own)) + dot_nt(grad_u, wide_half(1, own))
+        r.s_own[0, here] = back
+        r.s_own[1, here] = dot_nt(shared_h, wide_half(2, own))
+        return carry
+
+    lax.fori_loop(0, micro, shared_step, 0)
+    for swap_b in core_b:
+        swap_b.send()
+    for i, (rows_a, rows_b) in enumerate(((r.n_two, 0), (r.n_two, 1), (r.cot, 2))):
+        grads = dot_tn(rows_a[...], r.s_grads[rows_b])
+        r.sh_part[i] = grads.astype(BF).reshape(n, depth, shared)
+    sum_sh = [
+        Scatter(net, lambda b, i=i: r.sh_part.at[i, b], r.sh_fx.at[i], r.sh_fz.at[i])
+        for i in range(3)
+    ]
+
+    saves = []
+
+    def all_slots(ref, cut):
+        return ref[..., cut].reshape(micro * n * cap, -1)
+
+    def save(source, target, i):
+        copy = pltpu.make_async_copy(source, target, r.save_sems.at[i])
+        copy.start()
+        saves.append(copy)
+
+    for h, cut in enumerate(halves):
+        for i, (target, grads) in enumerate(((r.deg, r.e_dg), (r.deu, r.e_du))):
+            if h == 1:
+                saves[i].wait()
+            r.stage[i] = dot_tn(all_slots(r.x_in, cut), all_slots(grads, slice(None)))
+            save(r.stage.at[i], target.at[cut], 2 * h + i)
+        if h == 1:
+            saves[2].wait()
+        r.stage_d[...] = dot_tn(all_slots(r.e_h, slice(None)), all_slots(r.c_in, cut))
+        save(r.stage_d, r.ded.at[:, cut], 4 + h)
+
+    d_core = [Swap(net, r.d_tensor.at[m, 0], r.d_tensor.at[m, 1], net.other_core()) for m in micros]
+    d_y = [Swap(net, r.d_tensor.at[m, 2], r.d_tensor.at[m, 3], net.across_y()) for m in micros]
+    eight = iota((8, 128), 0)
+    d_rows = []
+    for m in micros:
+        send_d[m].finish()
+        line = jnp.zeros((8, 128), F32)
+        for b in range(n):
+            line = line + jnp.where(eight == b, r.d_in[m, b], 0.0)
+        d_rows.append(line)
+        d_core[m].start(line)
+    shared_grad = r.s_own[0] + core_b[0].other()
+    for m in micros:
+        d_y[m].start(d_rows[m] + d_core[m].other())
+    for m in micros:
+        send_g[m].finish()
+        moe_grad = dot(r.choice[m], r.g_in[m].reshape(n * cap, half))
+        y_swap[1][m].start(moe_grad + shared_grad[rows_of(m)])
+    for m in micros:
+        return_y(m)
+    grad_logits = []
+    for m in micros:
+        d_all = d_y[m].both()
+        grad_gate = jnp.zeros((local, 16), F32)
+        for b in range(n):
+            picked = r.choice_wide[m, :, b * 128 : (b + 1) * 128].astype(F32) * d_all[b : b + 1]
+            grad_gate = jnp.where(lane == b, jnp.sum(picked, axis=1, keepdims=True), grad_gate)
+        inner = jnp.sum(gates[m] * grad_gate, axis=1, keepdims=True)
+        grad_logits.append((gates[m] * (grad_gate - inner)).astype(BF))
+        share_b[m].start(y_swap[1][m].both())
+
+    w_qo = r.w_qo[...].reshape(model, wide)
+    kv_sums, grad_queries, gain_rows = [], [], []
+    for m in micros:
+        grad_two = share_b[m].finish() + dot(grad_logits[m], ext_low)
+        res = r.res[m]
+        cot = r.cot[rows_of(m)].astype(F32)
+        grad_res = cot + norm_back(grad_two, res, scale_two[m], gain_two)
+        r.gtok[rows_of(m)] = grad_res
+        gain_rows.append(jnp.sum(grad_two * res * scale_two[m], axis=0, keepdims=True))
+        kv_rows = r.kv[m].reshape(tree, wide)
+        total = r.total[m]
+        gm = by_head(dot(grad_res.astype(BF), w_qo), v_masks)
+        mixed = jnp.concatenate([r.mixed[m]] * heads, axis=0)
+        delta = jnp.sum(gm * mixed, axis=1, keepdims=True) / total
+        grad_summed = (gm / total).astype(BF)
+        expo = r.expo[m]
+        ds = (expo * (dot_nt(grad_summed, kv_rows) - delta)).astype(BF)
+        grad_kv = dot_tn(ds, r.q_rows[m]) * score_scale + dot_tn(expo.astype(BF), grad_summed)
+        r.kv_part[m] = grad_kv.astype(BF).reshape(n, local, wide)
+        kv_sums.append(
+            Scatter(net, lambda b, m=m: r.kv_part.at[m, b], r.kv_fx.at[m], r.kv_fz.at[m])
+        )
+        kv_sums[m].start()
+        grad_queries.append(join_heads(dot(ds, kv_rows), q_masks) * score_scale)
+
+    cosine, sine = turns(me)
+
+    def turned_back(grad):
+        return (grad * cosine - dot(grad, swap, EXACT) * sine).astype(BF)
+
+    for m in micros:
+        kv_sums[m].forward()
+    grad_q = turned_back(jnp.concatenate(grad_queries, axis=0))
+    grad_attn = r.gtok[...].astype(BF)
+    part_qo = dot_tn(r.n_one[...], grad_q) + dot_tn(grad_attn, r.mixed_low[...])
+    r.w_part[0] = part_qo.astype(BF).reshape(n, depth, wide)
+    sum_w = [
+        Scatter(net, lambda b, i=i: r.w_part.at[i, b], r.w_fx.at[i], r.w_fz.at[i])
+        for i in range(2)
+    ]
+    sum_w[0].start()
+
+    shared_y = r.s_own[1] + core_b[1].other()
+    for m in micros:
+        send_y[m].finish()
+        gate_wide = dot(gates[m], spread(cap).astype(F32), EXACT)
+        gate_high = gate_wide.astype(BF).astype(F32)
+        pick = r.choice[m].astype(F32)
+        y_rows = r.y_in[m].reshape(n * cap, half)
+        moe_y = dot((pick * gate_high).astype(BF), y_rows)
+        moe_y = moe_y + dot((pick * (gate_wide - gate_high)).astype(BF), y_rows)
+        y_swap[2][m].start(moe_y + shared_y[rows_of(m)])
+    for g in sum_sh:
+        g.start()
+
+    def weight_half(ref, h):
+        return ref[pl.ds(h * (n // 2), n // 2)].reshape(half, wide)
+
+    grad_kvs = []
+    for m in micros:
+        total = kv_sums[m].finish()
+        cos_m, sin_m = cosine[rows_of(m)], sine[rows_of(m)]
+        grad_kv = (total * cos_m - dot(total, swap, EXACT) * sin_m).astype(BF)
+        grad_kvs.append(grad_kv)
+        q_m = grad_q[rows_of(m)]
+        other = dot_nt(q_m, weight_half(r.w_qo, 1 - core))
+        core_c[m].start(other + dot_nt(grad_kv, weight_half(r.w_kv, 1 - core)))
+    for m in micros:
+        mine = dot_nt(grad_q[rows_of(m)], weight_half(r.w_qo, core))
+        mine = mine + dot_nt(grad_kvs[m], weight_half(r.w_kv, core))
+        y_swap[3][m].start(mine + core_c[m].other())
+    part_kv = dot_tn(r.n_one[...], jnp.concatenate(grad_kvs, axis=0))
+    r.w_part[1] = part_kv.astype(BF).reshape(n, depth, wide)
+    sum_w[1].start()
+    sum_w[0].forward()
+    for m in micros:
+        share_c[m].start(y_swap[3][m].both())
+    for m in micros:
+        res_half = jnp.where(core == 0, r.res[m, :, :half], r.res[m, :, half:])
+        share_out[m].start(res_half + y_swap[2][m].both())
+    sum_w[1].forward()
+    for g in sum_sh:
+        g.forward()
+
+    gain_one_row = jnp.zeros((1, model), F32)
+    for m in micros:
+        grad_one = share_c[m].finish()
+        tok = r.tok[rows_of(m)].astype(F32)
+        scale_one = norm_scale(tok)
+        r.gtok[rows_of(m)] += norm_back(grad_one, tok, scale_one, gain_one)
+        gain_one_row = gain_one_row + jnp.sum(grad_one * tok * scale_one, axis=0, keepdims=True)
+    grad_router = jnp.zeros((16, model), F32)
+    for m in micros:
+        grad_router = grad_router + dot_tn(grad_logits[m], r.n_two[rows_of(m)])
+    line = iota((16, model), 0)
+    small = jnp.where(line == 0, gain_one_row, grad_router)
+    small = jnp.where(line == 1, gain_rows[0] + gain_rows[1], small)
+    for b in range(n):
+        r.gains_out[b] = dot_nt(small, lay(b).astype(F32), EXACT)
+    send_gains = Exchange(net, lambda b: r.gains_out.at[b], lambda b: r.gains_in.at[b])
+    send_gains.start()
+    r.gains_in[me] = r.gains_out[me]
+    for m in micros:
+        r.out[rows_of(m)] = share_out[m].finish()
+
+    qo = sum_w[0].finish()
+    r.dwq[...] = dot_nt(qo, left.astype(F32), EXACT)
+    depth_eye = (iota((depth, depth), 0) == iota((depth, depth), 1)).astype(F32)
+    r.dwo[...] = dot_tn(dot_nt(qo, right.astype(F32), EXACT), depth_eye, EXACT)
+    kv = sum_w[1].finish()
+    r.dwk[...] = dot_nt(kv, left.astype(F32), EXACT)
+    r.dwv[...] = dot_nt(kv, right.astype(F32), EXACT)
+    for i, target in enumerate((r.dsg, r.dsu, r.dsd)):
+        target[...] = sum_sh[i].finish()
+    send_gains.finish()
+    gains = jnp.zeros((16, 128), F32)
+    for b in range(n):
+        gains = gains + r.gains_in[b]
+    r.dga[...] = gains[0:1, :depth]
+    r.dgb[...] = gains[1:2, :depth]
+    r.drouter[...] = gains[8:16, :depth]
+    for copy in saves[3:]:
+        copy.wait()
+    net.drain()
+
+
+def settle_kernel(count, *refs):
+    sources, targets, sems = refs[:count], refs[count : 2 * count], refs[2 * count]
+    copies = [
+        pltpu.make_async_copy(a, b, sems.at[i]) for i, (a, b) in enumerate(zip(sources, targets))
+    ]
+    for copy in copies:
+        copy.start()
+    for copy in copies:
+        copy.wait()
+
+
+def fits(mesh):
+    return mesh.shape["expert"] == 8 and mesh.shape["tensor"] == 4
+
+
+def fused_body(
+    tokens,
+    out_grad,
+    routes,
+    lengths,
+    parents,
+    attn_gain,
+    ffn_gain,
+    w_query,
+    w_key,
+    w_value,
+    w_out,
+    router,
+    shared_gate,
+    shared_up,
+    shared_down,
+    expert_gate,
+    expert_up,
+    expert_down,
+):
+    micro, local, model = tokens.shape
+    n = lax.axis_size("expert")
+    experts = router.shape[1]
+    depth, width = w_query.shape
+    hidden, shared = expert_gate.shape[2], shared_gate.shape[1]
+    s = types.SimpleNamespace(
+        n=n,
+        micro=micro,
+        local=local,
+        half=model // 2,
+        depth=depth,
+        width=width,
+        heads=width // HEAD,
+        hidden=hidden,
+        shared=shared,
+        cap=4 * local // experts,
+        segs=lengths.shape[1],
+    )
+    rows = micro * local
+    scratch = scratch_shapes(s)
+    names = PLACES + RESULTS + list(scratch)
+    shape = jax.ShapeDtypeStruct
+    vmem, smem = pl.BlockSpec(memory_space=pltpu.VMEM), pl.BlockSpec(memory_space=pltpu.SMEM)
+    hbm = pl.BlockSpec(memory_space=pl.ANY)
+    results = (
+        shape((rows, model), BF),
+        shape((rows, model), F32),
+        shape((1, depth), F32),
+        shape((1, depth), F32),
+        shape((depth, width), F32),
+        shape((depth, width), F32),
+        shape((depth, width), F32),
+        shape((width, depth), F32),
+        shape((experts, depth), F32),
+        shape((depth, shared), F32),
+        shape((depth, shared), F32),
+        shape((depth, shared), F32),
+        shape((model, hidden), F32),
+        shape((model, hidden), F32),
+        shape((hidden, model), F32),
+    )
+    found = pl.pallas_call(
+        functools.partial(layer_kernel, s, names),
+        out_shape=results,
+        in_specs=[vmem] * 3 + [smem] * 2 + [vmem] * 13,
+        out_specs=[vmem] * 12 + [hbm] * 3,
+        scratch_shapes=list(scratch.values()),
+        compiler_params=pltpu.CompilerParams(
+            collective_id=0, has_side_effects=True, vmem_limit_bytes=VMEM_LIMIT
+        ),
+    )(
+        tokens.reshape(rows, model),
+        out_grad.reshape(rows, model),
+        routes.transpose(0, 2, 1).reshape(2 * micro, local),
+        lengths,
+        parents,
+        attn_gain.reshape(1, depth),
+        ffn_gain.reshape(1, depth),
+        w_query,
+        w_key,
+        w_value,
+        w_out,
+        router.T,
+        shared_gate,
+        shared_up,
+        shared_down.T,
+        expert_gate[0],
+        expert_up[0],
+        expert_down[0],
+    )
+    settled = pl.pallas_call(
+        functools.partial(settle_kernel, len(results)),
+        out_shape=results,
+        in_specs=[vmem] * len(results),
+        out_specs=[hbm] * len(results),
+        scratch_shapes=[pltpu.SemaphoreType.DMA((len(results),))],
+        compiler_params=pltpu.CompilerParams(vmem_limit_bytes=VMEM_LIMIT),
+    )(*found)
+    out, gtok, dga, dgb, dwq, dwk, dwv, dwo, drouter, dsg, dsu, dsd, deg, deu, ded = settled
+    return (
+        out.reshape(micro, local, model),
+        gtok.reshape(micro, local, model),
+        dga.reshape(depth),
+        dgb.reshape(depth),
+        dwq,
+        dwk,
+        dwv,
+        dwo,
+        drouter.T,
+        dsg,
+        dsu,
+        dsd.T,
+        deg[None],
+        deu[None],
+        ded[None],
+    )
+
+
 def solution(mesh):
     in_specs = (
         P(None, "expert", None),
@@ -497,4 +1616,5 @@
         P("expert", None, "tensor"),
         P("expert", "tensor", None),
     )
-    return jax.shard_map(body, mesh=mesh, in_specs=in_specs, out_specs=out_specs, check_vma=False)
+    chosen = fused_body if fits(mesh) else plain_body
+    return jax.shard_map(chosen, mesh=mesh, in_specs=in_specs, out_specs=out_specs, check_vma=False)

time: 1400 us -> 234 us (0.17)
  waiting for transfers between devices: 747 us -> 0 us
  blocking collectives: 410 us -> 0 us
  Pallas kernels: 0 us -> 233 us
  matrix products: 74.7 us -> 0 us
  local copies, waits for them, and re-layouts: 56.4 us -> 0 us
  other arithmetic: 47.4 us -> 0 us
  starting transfers between devices: 35.3 us -> 0 us
  between operations: 18.2 us -> 0.84 us
    reduce_scatter x8 -> x0, waiting for transfers between devices: 484 us -> none  [the longest x2 110 us: body(): lax.psum_scatter(key_terms.reshape(tree_rows, 2 * local_width), 'expert',...]
    all_gather x10 -> x0, blocking collectives: 361 us -> none  [the longest x1 59.4 us: body(): lax.all_gather(shared_gate, 'expert', axis=0, tiled=True)]
    pallas_call x0 -> x2, Pallas kernels: none -> 233 us  [the longest x1 227 us: fused_body(): pl.pallas_call(functools.partial(layer_kernel, s, names), out_shape=resul...]
    unnamed x15 -> x0, waiting for transfers between devices: 97.7 us -> none
    psum x3 -> x0, waiting for transfers between devices: 94.4 us -> none  [the longest x1 33.3 us: body(): lax.psum((shared_y + moe_part).astype(jnp.bfloat16), 'tensor')]
    dot_general x80 -> x0, matrix products: 74.7 us -> none  [the longest x68 65.8 us: matmul(): return jnp.dot(left, right, preferred_element_type=jnp.float32)]
    all_to_all x8 -> x0, waiting for transfers between devices: 71.2 us -> none  [the longest x2 29.1 us: body(): lax.all_to_all(to_owners(grad_pairs_out, source), 'expert', split_axis=0,...]
    unnamed x2 -> x0, blocking collectives: 43.4 us -> none
  transfers between devices with their start and end apart: 21 -> 0, of which waited for: 18 -> 0; matrix products, arithmetic and copies ran while one was open for 8% -> 0% of each run, Pallas kernels for 0% -> 0%
where the time goes in v2:
time: 234 us
  Pallas kernels  233 us (100%)
    pallas_call x1, Pallas kernels, fused_body(): pl.pallas_call(functools.partial(layer_kernel, s, names), out_shape=resul...  227 us
    pallas_call x1, Pallas kernels, fused_body(): pl.pallas_call(functools.partial(settle_kernel, len(results)), out_shape=...  6.11 us

profile of v2, /device:TPU:0, one launch (start us, length us, event | category | flops | bytes accessed | tf_op | source)
XLA Modules:
  0.0 233.9 jit_solution(17327378614749081009)
XLA Ops:
  0.7 227.0 %shard_map.289 = (bf16[256,768]{1,0:T(8,128)(2,1)}, f32[256,768]{1,0:T(8,128)}, f32[1,96]{1,0:T(1,128)}, f32[1,96]{1,0:T(1,128)}, f32[96,192]{1,0:T(8,128)}, /*i...) custom-call(bf16[256,768]{1,0:T(8,128)(2,1)} %bitcast.24, ...), custom_call_target="tpu_custom_call" | custom-call | tf_op jit(solution)/shard_map/pallas_call | solution.py:1524
  227.7 6.1 %shard_map.290 = (bf16[256,768]{1,0:T(8,128)(2,1)}, f32[256,768]{1,0:T(8,128)}, f32[1,96]{1,0:T(1,128)}, f32[1,96]{1,0:T(1,128)}, f32[96,192]{1,0:T(8,128)}, /*i...) custom-call(bf16[256,768]{1,0:T(8,128)(2,1)} %get-tuple-element.45.r, ...), custom_call_target="tpu_custom_call" | custom-call | tf_op jit(solution)/shard_map/pallas_call | solution.py:1553

commit v3 on v2

--- a/solution.py
+++ b/solution.py
@@ -505,6 +505,7 @@
         self.send_sems = send_sems
         self.recv_sems = recv_sems
         self.sends = 0
+        self.free = []
         self.recvs = 0
         self.open = []
 
@@ -516,21 +517,24 @@
     def ids(self, to):
         return {"expert": to[0], "tensor": to[1]}
 
-    def push(self, src, dst, to, slot, when=None):
+    def push(self, src, dst, to, slot, when=None, bulk=False):
+        if not self.free:
+            self.free.append(self.sends)
+            self.sends += 1
+        send = self.free.pop(0)
         copy = pltpu.make_async_remote_copy(
             src_ref=src,
             dst_ref=dst,
-            send_sem=self.send_sems.at[self.sends],
+            send_sem=self.send_sems.at[send],
             recv_sem=self.recv_sems.at[slot],
             device_id=self.ids(to),
             device_id_type=MESH,
         )
-        self.sends += 1
         if when is None:
             copy.start()
         else:
             pl.when(when)(copy.start)
-        self.open.append((copy, when))
+        self.open.append((copy, when, send, bulk))
 
     def landed(self, dst, slot, when=None):
         copy = pltpu.make_async_remote_copy(
@@ -546,14 +550,15 @@
         else:
             pl.when(when)(copy.wait_recv)
 
-    def drain(self, first=0, last=None):
-        last = len(self.open) if last is None else last
-        for copy, when in self.open[first:last]:
-            if when is None:
-                copy.wait_send()
-            else:
-                pl.when(when)(copy.wait_send)
-        self.open[first:last] = []
+    def drain(self, bulk=True):
+        for copy, when, send, is_bulk in self.open:
+            if bulk or not is_bulk:
+                if when is None:
+                    copy.wait_send()
+                else:
+                    pl.when(when)(copy.wait_send)
+                self.free.append(send)
+        self.open = [one for one in self.open if one[3] and not bulk]
 
     def other_core(self):
         return (self.e, self.t + 1 - 2 * self.core)
@@ -628,7 +633,11 @@
         for d in range(1, net.nz + 1):
             zz = (net.z + d) % net.nz
             net.push(
-                self.block(zz * 2 + 1 - net.x), self.from_x.at[zz], net.across_x(), self.slot_x + zz
+                self.block(zz * 2 + 1 - net.x),
+                self.from_x.at[zz],
+                net.across_x(),
+                self.slot_x + zz,
+                bulk=True,
             )
 
     def forward(self):
@@ -790,6 +799,7 @@
         mixed=vm((micro, local, wide), F32),
         mixed_low=vm((micro * local, wide), BF),
         choice=vm((micro, local, n * cap), BF),
+        choice_half=vm((micro, local, n * cap // 2), BF),
         choice_wide=vm((micro, local, n * 128), BF),
         res=vm((micro, local, model), F32),
         n_one=vm((micro * local, model), BF),
@@ -806,7 +816,8 @@
         e_du=vm((micro, n * cap, hidden), BF),
         y_core=vm((micro, n, cap, half), BF),
         g_core=vm((micro, n, cap, half), BF),
-        y_in=vm((micro, n, cap, half), BF),
+        y_in=vm((micro, n, cap // 2, half), BF),
+        y_far=vm((micro, n, cap // 2, half), BF),
         g_in=vm((micro, n, cap, half), BF),
         d_out=vm((micro, n, 8, 128), F32),
         d_in=vm((micro, n, 8, 128), F32),
@@ -840,8 +851,8 @@
     )
 
 
-SENDS = 400
-RECVS = 400
+SENDS = 200
+RECVS = 300
 
 
 def layer_kernel(s, names, *refs):
@@ -918,6 +929,7 @@
             return (dot(rank, spread(span)) == wanted.astype(F32)).astype(BF)
 
         r.choice[m] = taken(cap)
+        r.choice_half[m] = taken(cap // 2, y * (cap // 2))
         r.choice_wide[m] = taken(128)
         quarter.append(taken(part, (core * 2 + y) * part))
         hit_rows = dot_tn(hits.astype(BF), r.choice_wide[m]).astype(BF)
@@ -1023,6 +1035,9 @@
         for m in micros:
             r.kv[m, b] = both[rows_of(m)]
 
+    get_qo.finish()
+    for g in get_sh:
+        g.start()
     key_value(me)
 
     def key_value_step(d, carry):
@@ -1032,7 +1047,6 @@
         return carry
 
     lax.fori_loop(1, n, key_value_step, 0)
-    get_qo.finish()
     r.n_one[...] = normed(r.tok[...])
     w_qo = r.w_qo[...].reshape(model, wide)
     cosine, sine = turns(me)
@@ -1040,10 +1054,8 @@
     queries = dot(r.n_one[...], w_qo) * cosine
     queries = queries + dot(r.n_one[...], dot(w_qo, swap_low).astype(BF)) * sine
     queries = queries.astype(BF)
-    for m in micros:
-        send_c[m].start()
-        send_h[m].start()
-    get_sh[0].start()
+    for g in get_sh:
+        g.step(1)
 
     head_of = iota((1, wide), 1) // HEAD
     q_masks = [head_of == h for h in range(heads)]
@@ -1095,14 +1107,21 @@
         r.mixed[m] = mixed
         r.mixed_low[rows_of(m)] = mixed.astype(BF)
         core_a[m].start(dot_nt(r.mixed_low[rows_of(m)], o_half(1 - core)))
+        if m == 0:
+            for g in get_sh:
+                g.step(2)
     for m in micros:
         mine = dot_nt(r.mixed_low[rows_of(m)], o_half(core))
         y_swap[0][m].start(mine + core_a[m].other())
-    get_sh[0].step(1)
+    for m in micros:
+        send_c[m].start()
+        send_h[m].start()
+    for g in get_sh:
+        g.step(3)
+    for m in micros:
+        share_a[m].start(y_swap[0][m].both())
     for m in micros:
         send_c[m].relay_y()
-    for m in micros:
-        share_a[m].start(y_swap[0][m].both())
 
     send_x = [Dispatch(net, r.x_out.at[m], r.x_in.at[m]) for m in micros]
     scale_two = []
@@ -1126,108 +1145,7 @@
         gates.append(chosen / (e_one + e_two))
     for m in micros:
         send_c[m].relay_core()
-    get_sh[0].step(2)
-    get_sh[0].step(3)
-    for m in micros:
-        send_x[m].relay_y()
-    get_sh[1].start()
-    get_sh[2].start()
-    for m in micros:
-        send_x[m].relay_core()
-    for m in micros:
-        send_h[m].finish()
-        send_c[m].finish()
-
-    slot_gc = net.recv_slots(micro)
-    slot_yc = net.recv_slots(micro)
-    send_g = [
-        Exchange(net, lambda b, m=m: r.g_core.at[m, b], lambda b, m=m: r.g_in.at[m, b])
-        for m in micros
-    ]
-    send_y = [
-        Exchange(net, lambda b, m=m: r.y_core.at[m, b], lambda b, m=m: r.y_in.at[m, b])
-        for m in micros
-    ]
-    send_d = [
-        Exchange(net, lambda b, m=m: r.d_out.at[m, b], lambda b, m=m: r.d_in.at[m, b])
-        for m in micros
-    ]
-    slot_eye = eye[:cap]
-    slot_line = iota((cap, 128), 0) == iota((cap, 128), 1)
-    own_lane = iota((n * cap, 16), 1) - 8 == me
-    group = 4
-    halves = [slice(0, half), slice(half, model)]
-
-    def expert(m):
-        x_rows = r.x_in[m].reshape(n * cap, model)
-        z_all = dot_nt(x_rows, ext_low)
-        hit = jnp.concatenate([dot_nt(slot_eye, r.h_in[m, b]) for b in range(n)], axis=0)
-        z_own = jnp.sum(jnp.where(own_lane, z_all, 0.0), axis=1, keepdims=True)
-        z_other = jnp.sum(jnp.where(own_lane, 0.0, z_all * hit), axis=1, keepdims=True)
-        z_top = jnp.maximum(z_own, z_other)
-        e_own, e_other = jnp.exp(z_own - z_top), jnp.exp(z_other - z_top)
-        r.gate_col[m] = e_own / (e_own + e_other)
-        count = group * cap
-
-        def step(i, carry):
-            span = pl.ds(i * group, group)
-            flat = pl.ds(pl.multiple_of(i * count, count), count)
-            x = r.x_in[m, span].reshape(count, model)
-            c = r.c_in[m, span].reshape(count, model)
-            gate = r.gate_col[m, flat]
-            gate_pre = dot(x, r.eg[...])
-            up_pre = dot(x, r.eu[...])
-            act, slope = silu_both(gate_pre)
-            hid = (act * up_pre).astype(BF)
-            grad_y = (gate * c.astype(F32)).astype(BF)
-            grad_hid = dot_nt(grad_y, r.ed[...])
-            grad_g = (grad_hid * up_pre * slope).astype(BF)
-            grad_u = (grad_hid * act).astype(BF)
-            r.e_h[m, flat] = hid
-            r.e_dg[m, flat] = grad_g
-            r.e_du[m, flat] = grad_u
-            dots = jnp.zeros((count, 1), F32)
-            for cut in halves:
-                out = dot(hid, r.ed[:, cut])
-                r.tok_all[span, 0, m, :, cut] = out.astype(BF).reshape(group, cap, half)
-                dots = dots + jnp.sum(out * c[:, cut].astype(F32), axis=1, keepdims=True)
-                back = dot_nt(grad_g, r.eg[cut]) + dot_nt(grad_u, r.eu[cut])
-                r.tok_all[span, 1, m, :, cut] = back.astype(BF).reshape(group, cap, half)
-            r.c_in[m, span] = grad_y.reshape(group, 2, 2, part, model)
-            for b in range(group):
-                line = jnp.where(slot_line, dots[b * cap : (b + 1) * cap], 0.0)
-                line = jnp.sum(line, axis=0, keepdims=True)
-                r.d_out[m, i * group + b] = jnp.broadcast_to(line, (8, 128))
-            return carry
-
-        lax.fori_loop(0, n // group, step, 0)
-        net.push(r.tok_all.at[:, 1, m, :, other_half], r.g_core.at[m], net.other_core(), slot_gc + m)
-        net.push(r.tok_all.at[:, 0, m, :, other_half], r.y_core.at[m], net.other_core(), slot_yc + m)
-
-    def return_g(m):
-        send_d[m].start()
-        r.d_in[m, me] = r.d_out[m, me]
-        net.landed(r.g_core.at[m], slot_gc + m)
-        r.g_core[m] = (r.tok_all[:, 1, m, :, my_half].astype(F32) + r.g_core[m].astype(F32)).astype(BF)
-        send_g[m].start()
-        r.g_in[m, me] = r.g_core[m, me]
-
-    def return_y(m):
-        net.landed(r.y_core.at[m], slot_yc + m)
-        r.y_core[m] = (r.tok_all[:, 0, m, :, my_half].astype(F32) + r.y_core[m].astype(F32)).astype(BF)
-        send_y[m].start()
-        r.y_in[m, me] = r.y_core[m, me]
-
-    net.drain()
-    for m in micros:
-        send_x[m].finish()
-        expert(m)
-    for m in micros:
-        return_g(m)
-
-    for distance in range(1, net.nz):
-        get_sh[1].step(distance)
-        get_sh[2].step(distance)
+
     for g in get_sh:
         g.finish()
 
@@ -1267,6 +1185,116 @@
         for i in range(3)
     ]
 
+    for m in micros:
+        send_x[m].relay_y()
+    for m in micros:
+        send_x[m].relay_core()
+    for m in micros:
+        send_h[m].finish()
+        send_c[m].finish()
+
+    slot_gc = net.recv_slots(micro)
+    slot_yc = net.recv_slots(micro)
+    slot_yy = net.recv_slots(micro)
+    my_slots = pl.ds(pl.multiple_of(y * (cap // 2), cap // 2), cap // 2)
+    far_slots = pl.ds(pl.multiple_of((1 - y) * (cap // 2), cap // 2), cap // 2)
+    send_g = [
+        Exchange(net, lambda b, m=m: r.g_core.at[m, b], lambda b, m=m: r.g_in.at[m, b])
+        for m in micros
+    ]
+    send_y = [
+        Exchange(net, lambda b, m=m: r.y_core.at[m, b, my_slots], lambda b, m=m: r.y_in.at[m, b])
+        for m in micros
+    ]
+    send_d = [
+        Exchange(net, lambda b, m=m: r.d_out.at[m, b], lambda b, m=m: r.d_in.at[m, b])
+        for m in micros
+    ]
+    slot_eye = eye[:cap]
+    slot_line = iota((cap, 128), 0) == iota((cap, 128), 1)
+    own_lane = iota((n * cap, 16), 1) - 8 == me
+    group = 4
+    halves = [slice(0, half), slice(half, model)]
+
+    def expert_gates(m):
+        x_rows = r.x_in[m].reshape(n * cap, model)
+        z_all = dot_nt(x_rows, ext_low)
+        hit = jnp.concatenate([dot_nt(slot_eye, r.h_in[m, b]) for b in range(n)], axis=0)
+        z_own = jnp.sum(jnp.where(own_lane, z_all, 0.0), axis=1, keepdims=True)
+        z_other = jnp.sum(jnp.where(own_lane, 0.0, z_all * hit), axis=1, keepdims=True)
+        z_top = jnp.maximum(z_own, z_other)
+        e_own, e_other = jnp.exp(z_own - z_top), jnp.exp(z_other - z_top)
+        r.gate_col[m] = e_own / (e_own + e_other)
+
+    def expert_rows(m, i):
+        count = group * cap
+        span = slice(i * group, (i + 1) * group)
+        flat = slice(i * count, (i + 1) * count)
+        x = r.x_in[m, span].reshape(count, model)
+        c = r.c_in[m, span].reshape(count, model)
+        gate = r.gate_col[m, flat]
+        gate_pre = dot(x, r.eg[...])
+        up_pre = dot(x, r.eu[...])
+        act, slope = silu_both(gate_pre)
+        hid = (act * up_pre).astype(BF)
+        grad_y = (gate * c.astype(F32)).astype(BF)
+        grad_hid = dot_nt(grad_y, r.ed[...])
+        grad_g = (grad_hid * up_pre * slope).astype(BF)
+        grad_u = (grad_hid * act).astype(BF)
+        r.e_h[m, flat] = hid
+        r.e_dg[m, flat] = grad_g
+        r.e_du[m, flat] = grad_u
+        dots = jnp.zeros((count, 1), F32)
+        for cut in halves:
+            out = dot(hid, r.ed[:, cut])
+            r.tok_all[span, 0, m, :, cut] = out.astype(BF).reshape(group, cap, half)
+            dots = dots + jnp.sum(out * c[:, cut].astype(F32), axis=1, keepdims=True)
+            back = dot_nt(grad_g, r.eg[cut]) + dot_nt(grad_u, r.eu[cut])
+            r.tok_all[span, 1, m, :, cut] = back.astype(BF).reshape(group, cap, half)
+        r.c_in[m, span] = grad_y.reshape(group, 2, 2, part, model)
+        for b in range(group):
+            line = jnp.where(slot_line, dots[b * cap : (b + 1) * cap], 0.0)
+            line = jnp.sum(line, axis=0, keepdims=True)
+            r.d_out[m, i * group + b] = jnp.broadcast_to(line, (8, 128))
+
+    def expert_sent(m):
+        net.push(r.tok_all.at[:, 1, m, :, other_half], r.g_core.at[m], net.other_core(), slot_gc + m)
+        net.push(r.tok_all.at[:, 0, m, :, other_half], r.y_core.at[m], net.other_core(), slot_yc + m)
+
+    def return_g(m):
+        send_d[m].start()
+        r.d_in[m, me] = r.d_out[m, me]
+        net.landed(r.g_core.at[m], slot_gc + m)
+        r.g_core[m] = (r.tok_all[:, 1, m, :, my_half].astype(F32) + r.g_core[m].astype(F32)).astype(BF)
+        send_g[m].start()
+        r.g_in[m, me] = r.g_core[m, me]
+
+    def add_y(m):
+        net.landed(r.y_core.at[m], slot_yc + m)
+        mine = r.tok_all[:, 0, m, :, my_half].astype(F32)
+        r.y_core[m] = (mine + r.y_core[m].astype(F32)).astype(BF)
+        net.push(r.y_core.at[m, :, far_slots], r.y_far.at[m], net.across_y(), slot_yy + m)
+
+    def return_y(m):
+        net.landed(r.y_far.at[m], slot_yy + m)
+        both = r.y_core[m, :, my_slots].astype(F32) + r.y_far[m].astype(F32)
+        r.y_core[m, :, my_slots] = both.astype(BF)
+        send_y[m].start()
+        r.y_in[m, me] = r.y_core[m, me, my_slots]
+
+    net.drain()
+    sum_sh[0].start()
+    for m in micros:
+        send_x[m].finish()
+        expert_gates(m)
+        for i in range(n // group):
+            if m > 0 and i == 1:
+                return_g(m - 1)
+            expert_rows(m, i)
+        expert_sent(m)
+    return_g(micro - 1)
+    sum_sh[1].start()
+
     saves = []
 
     def all_slots(ref, cut):
@@ -1288,6 +1316,8 @@
         r.stage_d[...] = dot_tn(all_slots(r.e_h, slice(None)), all_slots(r.c_in, cut))
         save(r.stage_d, r.ded.at[:, cut], 4 + h)
 
+    for m in micros:
+        add_y(m)
     d_core = [Swap(net, r.d_tensor.at[m, 0], r.d_tensor.at[m, 1], net.other_core()) for m in micros]
     d_y = [Swap(net, r.d_tensor.at[m, 2], r.d_tensor.at[m, 3], net.across_y()) for m in micros]
     eight = iota((8, 128), 0)
@@ -1306,6 +1336,8 @@
         send_g[m].finish()
         moe_grad = dot(r.choice[m], r.g_in[m].reshape(n * cap, half))
         y_swap[1][m].start(moe_grad + shared_grad[rows_of(m)])
+    net.drain(bulk=False)
+    sum_sh[2].start()
     for m in micros:
         return_y(m)
     grad_logits = []
@@ -1318,6 +1350,8 @@
         inner = jnp.sum(gates[m] * grad_gate, axis=1, keepdims=True)
         grad_logits.append((gates[m] * (grad_gate - inner)).astype(BF))
         share_b[m].start(y_swap[1][m].both())
+
+    sum_sh[0].forward()
 
     w_qo = r.w_qo[...].reshape(model, wide)
     kv_sums, grad_queries, gain_rows = [], [], []
@@ -1364,15 +1398,14 @@
     shared_y = r.s_own[1] + core_b[1].other()
     for m in micros:
         send_y[m].finish()
-        gate_wide = dot(gates[m], spread(cap).astype(F32), EXACT)
+        gate_wide = dot(gates[m], spread(cap // 2).astype(F32), EXACT)
         gate_high = gate_wide.astype(BF).astype(F32)
-        pick = r.choice[m].astype(F32)
-        y_rows = r.y_in[m].reshape(n * cap, half)
+        pick = r.choice_half[m].astype(F32)
+        y_rows = r.y_in[m].reshape(n * cap // 2, half)
         moe_y = dot((pick * gate_high).astype(BF), y_rows)
         moe_y = moe_y + dot((pick * (gate_wide - gate_high)).astype(BF), y_rows)
         y_swap[2][m].start(moe_y + shared_y[rows_of(m)])
-    for g in sum_sh:
-        g.start()
+    sum_sh[1].forward()
 
     def weight_half(ref, h):
         return ref[pl.ds(h * (n // 2), n // 2)].reshape(half, wide)
@@ -1393,6 +1426,7 @@
     part_kv = dot_tn(r.n_one[...], jnp.concatenate(grad_kvs, axis=0))
     r.w_part[1] = part_kv.astype(BF).reshape(n, depth, wide)
     sum_w[1].start()
+    sum_sh[2].forward()
     sum_w[0].forward()
     for m in micros:
         share_c[m].start(y_swap[3][m].both())
@@ -1400,8 +1434,6 @@
         res_half = jnp.where(core == 0, r.res[m, :, :half], r.res[m, :, half:])
         share_out[m].start(res_half + y_swap[2][m].both())
     sum_w[1].forward()
-    for g in sum_sh:
-        g.forward()
 
     gain_one_row = jnp.zeros((1, model), F32)
     for m in micros:
@@ -1446,14 +1478,21 @@
 
 
 def settle_kernel(count, *refs):
-    sources, targets, sems = refs[:count], refs[count : 2 * count], refs[2 * count]
-    copies = [
-        pltpu.make_async_copy(a, b, sems.at[i]) for i, (a, b) in enumerate(zip(sources, targets))
+    sources, targets, stops = refs[:count], refs[count : 2 * count], refs[2 * count : 3 * count]
+    sems = refs[3 * count]
+    reads = [
+        pltpu.make_async_copy(a, b, sems.at[0, i]) for i, (a, b) in enumerate(zip(sources, stops))
     ]
-    for copy in copies:
-        copy.start()
-    for copy in copies:
-        copy.wait()
+    writes = [
+        pltpu.make_async_copy(a, b, sems.at[1, i]) for i, (a, b) in enumerate(zip(stops, targets))
+    ]
+    for read in reads:
+        read.start()
+    for read, write in zip(reads, writes):
+        read.wait()
+        write.start()
+    for write in writes:
+        write.wait()
 
 
 def fits(mesh):
@@ -1553,9 +1592,10 @@
     settled = pl.pallas_call(
         functools.partial(settle_kernel, len(results)),
         out_shape=results,
-        in_specs=[vmem] * len(results),
+        in_specs=[hbm] * len(results),
         out_specs=[hbm] * len(results),
-        scratch_shapes=[pltpu.SemaphoreType.DMA((len(results),))],
+        scratch_shapes=[pltpu.VMEM(one.shape, one.dtype) for one in results]
+        + [pltpu.SemaphoreType.DMA((2, len(results)))],
         compiler_params=pltpu.CompilerParams(vmem_limit_bytes=VMEM_LIMIT),
     )(*found)
     out, gtok, dga, dgb, dwq, dwk, dwv, dwo, drouter, dsg, dsu, dsd, deg, deu, ded = settled

time: 234 us -> 191 us (0.82)
  Pallas kernels: 233 us -> 190 us
    pallas_call x1, Pallas kernels: 227 us -> 184 us  [fused_body(): pl.pallas_call(functools.partial(layer_kernel, s, names), out_shape=resul...]
where the time goes in v3:
time: 191 us
  Pallas kernels  190 us (99%)
    pallas_call x1, Pallas kernels, fused_body(): pl.pallas_call(functools.partial(layer_kernel, s, names), out_shape=resul...  184 us
    pallas_call x1, Pallas kernels, fused_body(): pl.pallas_call(functools.partial(settle_kernel, len(results)), out_shape=...  5.82 us

profile of v3, /device:TPU:0, one launch (start us, length us, event | category | flops | bytes accessed | tf_op | source)
XLA Modules:
  0.0 190.9 jit_solution(15412962767375374053)
XLA Ops:
  0.7 184.2 %shard_map.289 = (bf16[256,768]{1,0:T(8,128)(2,1)}, f32[256,768]{1,0:T(8,128)}, f32[1,96]{1,0:T(1,128)}, f32[1,96]{1,0:T(1,128)}, f32[96,192]{1,0:T(8,128)}, /*i...) custom-call(bf16[256,768]{1,0:T(8,128)(2,1)} %bitcast.24, ...), custom_call_target="tpu_custom_call" | custom-call | tf_op jit(solution)/shard_map/pallas_call | solution.py:1563
  184.9 5.8 %shard_map.290 = (bf16[256,768]{1,0:T(8,128)(2,1)}, f32[256,768]{1,0:T(8,128)}, f32[1,96]{1,0:T(1,128)}, f32[1,96]{1,0:T(1,128)}, f32[96,192]{1,0:T(8,128)}, /*i...) custom-call(bf16[256,768]{1,0:T(8,128)(2,1)} %get-tuple-element.45.r, ...), custom_call_target="tpu_custom_call" | custom-call | tf_op jit(solution)/shard_map/pallas_call | solution.py:1592
